TPU v7x, 256 devices: a whole 4x4x8 slice. The times are simulated.
256 devices in a mesh: feat: 2 (over core), dom: 128 (over z, y, x).
Axes of the slice: x: 4, y: 4, z: 8, core: 2. Of those that a mesh axis runs over, the one named last changes fastest.
Arguments:
- features: bfloat16 [131072, 1024], P('dom', 'feat'), may hold values from -6 to 6
- tile_weight: bfloat16 [16384, 128, 128], P('dom'), may hold values from 0 to 0.029907227
- tile_dst: int32 [16384], P('dom'), may hold values from 0 to 127
- tile_src: int32 [16384], P('dom'), may hold values from 0 to 7
- tile_rows: int32 [16384], P('dom'), may hold values from 1 to 128
- w_self1: bfloat16 [1024, 256], P('feat'), may hold values from -0.1875 to 0.1875
- neighbour_weight_first: bfloat16 [1024, 256], P('feat'), may hold values from -0.1875 to 0.1875
- send_list: int32 [128, 128, 8], replicated, may hold values from 0 to 127
- send_count: int32 [128, 128], replicated, may hold values from 1 to 8
- adj_two: bfloat16 [8192, 1152], P('dom'), may hold values from 0 to 0.0049743652
- w_self2: bfloat16 [256, 172], replicated, may hold values from -0.375 to 0.375
- w_neigh2: bfloat16 [256, 172], replicated, may hold values from -0.375 to 0.375
Outputs:
- logits: float32 [8192, 172], P('dom')
Inputs may be any that keep to these rules, and one draw needn't show every extreme that they name: `send_list`: every send list slot names a local hidden row of the sender.
All inputs are finite; a program needn't handle non-finite values.
Results may differ from a plain program's by a relative error of at most 0.0012.
The roundings to bfloat16 on the way count: a program that leaves them out, or rounds other values in their place, can miss the bound.
Values may be sent and summed in bfloat16 or wider, within the bound.
A program may use at most 128 MiB of HBM per device.

v0:
```python
import jax
import jax.numpy as jnp
from jax import lax
from jax.sharding import PartitionSpec as P


def pull_rows(hidden, send_list, send_count):
    parts = lax.axis_size("dom")
    me = lax.axis_index("dom")
    width = hidden.shape[1]
    slot_count = send_list.shape[2]
    slots = jnp.arange(slot_count, dtype=jnp.int32)
    everything = lax.all_gather(hidden, "dom", axis=0, tiled=True)
    lists = lax.dynamic_slice_in_dim(send_list, me, 1, 1)[:, 0, :]
    counts = lax.dynamic_slice_in_dim(send_count, me, 1, 1)[:, 0]
    owners = jnp.arange(parts, dtype=jnp.int32)[:, None] * hidden.shape[0]
    rows = jnp.take(everything, (owners + lists).reshape(parts * slot_count), axis=0)
    rows = rows.reshape(parts, slot_count, width)
    valid = (slots[None, :] < counts[:, None])[:, :, None]
    rows = jnp.where(valid, rows, jnp.zeros_like(rows))
    return rows.reshape(parts * slot_count, width)


def body(
    features,
    tile_weight,
    tile_dst,
    tile_src,
    tile_rows,
    w_self1,
    neighbour_weight_first,
    send_list,
    send_count,
    adj_two,
    w_self2,
    w_neigh2,
):
    tile_size = tile_weight.shape[1]
    n_rows = features.shape[0]
    slice_width = features.shape[1]
    hidden_width = w_self1.shape[1]
    blocks = features.reshape(n_rows // tile_size, tile_size, slice_width)
    row_indices = jnp.arange(tile_size, dtype=jnp.int32)
    valid = row_indices[None, :, None] < tile_rows[:, None, None]
    masked_features = jnp.where(valid, tile_weight, jnp.zeros_like(tile_weight))
    source_nodes = jnp.take(blocks, tile_src, axis=0)
    collected_rows = jnp.einsum(
        "zvx,zxm->zvm", masked_features, source_nodes, preferred_element_type=jnp.float32
    ).astype(jnp.bfloat16)
    neighbour_rows = jnp.einsum(
        "kys,sj->kyj", collected_rows, neighbour_weight_first, preferred_element_type=jnp.float32
    )
    block_count = lax.axis_size("dom") * tile_size // tile_size
    targets = jnp.arange(block_count, dtype=jnp.int32)
    onehot = (tile_dst[:, None] == targets[None, :]).astype(jnp.float32)
    summed = jnp.einsum("tb,trh->brh", onehot, neighbour_rows, precision=lax.Precision.HIGHEST)
    scattered = lax.psum_scatter(
        summed.reshape(lax.axis_size("dom") * tile_size, hidden_width),
        "dom",
        scatter_dimension=0,
        tiled=True,
    )
    own_rows = features[:tile_size]
    total = scattered + jnp.dot(own_rows, w_self1, preferred_element_type=jnp.float32)
    out_rows = adj_two.shape[0]
    pre = lax.psum(total, "feat")
    hidden = jnp.maximum(pre, 0.0).astype(jnp.bfloat16)
    received = pull_rows(hidden, send_list, send_count)
    pool = jnp.concatenate([hidden, received], axis=0)
    neighbour_mean = jnp.dot(adj_two, pool, preferred_element_type=jnp.float32).astype(jnp.bfloat16)
    logits = jnp.dot(hidden[:out_rows], w_self2, preferred_element_type=jnp.float32) + jnp.dot(
        neighbour_mean, w_neigh2, preferred_element_type=jnp.float32
    )
    return logits


def solution(mesh):
    in_specs = (
        P("dom", "feat"),
        P("dom", None, None),
        P("dom"),
        P("dom"),
        P("dom"),
        P("feat", None),
        P("feat", None),
        P(),
        P(),
        P("dom", None),
        P(),
        P(),
    )
    out_specs = P("dom", None)
    return jax.shard_map(body, mesh=mesh, in_specs=in_specs, out_specs=out_specs, check_vma=False)
```

profile of v0, /device:TPU:1, one launch (start us, length us, event | category | flops | bytes accessed | tf_op | source)
XLA Modules:
  0.0 969.9 jit_solution(11735483360389867865)
XLA Ops:
  6.5 0.7 compare_select_fusion.2
  7.3 0.7 compare_and_fusion.1
  7.9 0.7 iota_compare_fusion.1
  8.7 9.5 gather_fusion
  18.1 15.8 %fusion.5 = bf16[128,128,512]{2,1,0:T(8,128)(2,1)} fusion(bf16[128,128,512]{2,1,0:T(8,128)(2,1)} %gather_fusion, pred[128]{0:T(512)(128)(4,1)S(1)} %compare_and_fusion.1, bf16[128,128,128]{2,1,0:T(8,128)(2,1)} %param.13, pred[128,128]{1,0:T(8,128)(4,1)S(1)} %iota_compare_fusion.1), kind=kOutput, calls=%fused_computation.7 | convolution fusion | flops 2166358016 | bytes 37765248 | tf_op jit(solution)/shard_map/zvx,zxm->zvm/dot_general | solution.py:47
  33.9 0.0 copy-done.1
  33.9 30.1 %fusion = f32[128,128,256]{2,0,1:T(8,128)} fusion(bf16[128,128,512]{2,1,0:T(8,128)(2,1)} %fusion.5, bf16[512,256]{1,0:T(8,128)(2,1)S(1)} %copy-done.1), kind=kOutput, calls=%fused_computation.2 | convolution fusion | flops 4294967296 | bytes 33816576 | tf_op jit(solution)/shard_map/kys,sj->kyj/dot_general | solution.py:50
  64.1 0.0 copy-done.5
  64.1 15.5 %fusion.23 = f32[128,128,256]{2,0,1:T(8,128)} fusion(f32[128,128,256]{2,0,1:T(8,128)} %fusion, s32[128]{0:T(128)S(1)} %copy-done.5), kind=kOutput, calls=%fused_computation.29 | convolution fusion | flops 6442467328 | bytes 33554944 | tf_op jit(solution)/shard_map/tb,trh->brh/dot_general | solution.py:56
  79.6 17.7 %copy.13 = f32[128,128,256]{2,1,0:T(8,128)} copy(f32[128,128,256]{2,0,1:T(8,128)} %fusion.23) | data formatting | bytes 33554432 | tf_op jit(solution)/shard_map/tb,trh->brh/dot_general | solution.py:56
  97.3 0.0 copy-start.7
  97.3 0.0 reduce-scatter.2.cloned.1.call-update
  97.3 0.0 all-gather.2.cloned.1.call-start
  97.4 639.1 %reduce-scatter.2.cloned.1.call-done = f32[128,256]{1,0:T(8,128)} async-done(((f32[16384,256]{1,0:T(8,128)}), f32[128,256]{1,0:T(8,128)}) %reduce-scatter.2.cloned.1.call-update) | async-done | bytes 131088 | tf_op jit(solution)/shard_map/reduce_scatter | solution.py:57
  736.5 1.2 convolution_add_fusion
  737.6 99.9 %all-reduce.1 = bf16[128,256]{1,0:T(8,128)(2,1)S(1)} all-reduce(f32[128,256]{1,0:T(8,128)S(1)} %convolution_add_fusion), channel_id=1, replica_groups=mesh['feat'=2,'dom'=128] {'feat'}, use_global_device_ids=true, to_apply=%region_1.2 | all-reduce | flops 32768 | bytes 196608 | tf_op jit(solution)/shard_map/psum | solution.py:66
  837.5 0.6 maximum_convert_fusion
  838.2 0.0 all-gather.2.cloned.1.call-update
  838.2 0.1 add.73
  838.3 0.1 add.78
  838.4 0.1 add.74
  838.5 2.4 dynamic-slice_reduce_fusion
  840.9 0.1 squeeze.6
  841.0 0.1 squeeze.5
  841.1 0.2 dynamic-slice_reduce_fusion.1
  841.3 0.1 iota_compare_fusion
  841.4 0.1 lt.83
  841.5 0.9 fusion.25
  842.4 110.3 %all-gather.2.cloned.1.call-done = bf16[16384,256]{1,0:T(8,128)(2,1)} async-done(((bf16[128,256]{1,0:T(8,128)(2,1)}), bf16[16384,256]{1,0:T(8,128)(2,1)}) %all-gather.2.cloned.1.call-update) | async-done | bytes 8388624 | tf_op jit(solution)/shard_map/all_gather | solution.py:13
  952.8 7.9 gather_fusion.1
  960.7 0.3 select_select_fusion
  961.1 2.0 fusion.13
  (19 shorter events, 0.1 us)
Async XLA Ops:
  6.5 832.0 %copy-start = (s32[128,128,8]{1,2,0:T(8,128)S(1)}, s32[128,128,8]{1,2,0:T(8,128)}, u32[]{:S(2)}) copy-start(s32[128,128,8]{1,2,0:T(8,128)} %param.19) | copy-start | bytes 1572868
  6.5 729.9 %reduce-scatter.2.cloned.1.call-start = ((), (), s32[]{:S(2)}) async-start(), calls=%async_computation.1 | async-start | bytes 16908288 | tf_op jit(solution)/shard_map/reduce_scatter | solution.py:57
  18.1 15.8 %copy-start.1 = (bf16[512,256]{1,0:T(8,128)(2,1)S(1)}, bf16[512,256]{1,0:T(8,128)(2,1)}, u32[]{:S(2)}) copy-start(bf16[512,256]{1,0:T(8,128)(2,1)} %param.18) | copy-start | bytes 786436
  33.9 30.1 %copy-start.5 = (s32[128]{0:T(128)S(1)}, s32[128]{0:T(128)}, u32[]{:S(2)}) copy-start(s32[128]{0:T(128)} %param.14) | copy-start | bytes 1540
  97.3 639.2 %copy-start.2 = (bf16[512,256]{1,0:T(8,128)(2,1)S(1)}, bf16[512,256]{1,0:T(8,128)(2,1)}, u32[]{:S(2)}) copy-start(bf16[512,256]{1,0:T(8,128)(2,1)} %param.17) | copy-start | bytes 786436
  97.3 743.8 %copy-start.4 = (s32[128,128]{1,0:T(8,128)S(1)}, s32[128,128]{1,0:T(8,128)}, u32[]{:S(2)}) copy-start(s32[128,128]{1,0:T(8,128)} %param.20) | copy-start | bytes 196612
  97.3 744.2 %copy-start.3 = (bf16[256,172]{0,1:T(8,128)(2,1)S(1)}, bf16[256,172]{0,1:T(8,128)(2,1)}, u32[]{:S(2)}) copy-start(bf16[256,172]{0,1:T(8,128)(2,1)} %param.22) | copy-start | bytes 264196
  97.3 863.8 %copy-start.6 = (bf16[64,1152]{1,0:T(8,128)(2,1)S(1)}, bf16[64,1152]{1,0:T(8,128)(2,1)}, u32[]{:S(2)}) copy-start(bf16[64,1152]{1,0:T(8,128)(2,1)} %param.21) | copy-start | bytes 442372
  97.3 863.8 %copy-start.7 = (bf16[256,172]{0,1:T(8,128)(2,1)S(1)}, bf16[256,172]{0,1:T(8,128)(2,1)}, u32[]{:S(2)}) copy-start(bf16[256,172]{0,1:T(8,128)(2,1)} %param.23) | copy-start | bytes 264196
  97.3 855.4 %all-gather.2.cloned.1.call-start = ((), (), s32[]{:S(2)}) async-start(), calls=%async_computation.2 | async-start | bytes 8454144 | tf_op jit(solution)/shard_map/all_gather | solution.py:13
Sparse Core Ops, SparseCore 0:
  97.5 638.9 reduce-scatter.1
  838.3 114.4 all-gather.1
where the time goes:
time: 972 us; the launch traced here: 970 us
  waiting for transfers between devices  749 us (77%)
  blocking collectives  99.9 us (10%)
  matrix products  65.5 us (7%)
  local copies, waits for them, and re-layouts  38.3 us (4%)
  between operations  13.6 us (1%)
    reduce_scatter x1, waiting for transfers between devices, body(): lax.psum_scatter(summed.reshape(lax.axis_size('dom') * tile_size, hidden_...  639 us
    all_gather x1, waiting for transfers between devices, pull_rows(): everything = lax.all_gather(hidden, 'dom', axis=0, tiled=True)  110 us
    psum x1, blocking collectives, body(): pre = lax.psum(total, 'feat')  99.9 us
    dot_general x1, matrix products, body(): jnp.einsum('kys,sj->kyj', collected_rows, neighbour_weight_first, preferr...  30.1 us
  transfers between devices with their start and end apart: 2, of which 2 were waited for; matrix products, arithmetic and copies ran while one was open for 0% of the time, Pallas kernels for 0%

commit v1 on v0

v1 whole, which is shorter than its diff:
```python
import functools

import jax
import jax.numpy as jnp
import numpy as np
from jax import lax
from jax.experimental import pallas as pl
from jax.experimental.pallas import tpu as pltpu
from jax.sharding import PartitionSpec as P

DIMS = {128: (4, 4, 8), 16: (4, 2, 2)}
SHARES = ((0, 24), (24, 24), (48, 16))
ORDERS = ((0, 1, 2), (1, 0, 2), (2, 0, 1))
GROUP = 4
VMEM_LIMIT = 56 * 1024 * 1024
MESH = pl.DeviceIdType.MESH


def bits_of(count):
    return count.bit_length() - 1


def steps_of(parts, share):
    dims = DIMS[parts]
    return [(axis, i) for axis in ORDERS[share] for i in range(bits_of(dims[axis]))]


def chunk_of(parts):
    return parts // 8


def packed_from(parts):
    return 8 if parts >= 128 else 2


@functools.lru_cache(maxsize=None)
def slot_table(parts):
    nx, ny, nz = DIMS[parts]
    table = np.zeros((2, len(SHARES), parts), np.int32)
    for f in range(2):
        for share in range(len(SHARES)):
            for b in range(parts):
                coords = (b % nx, b // nx % ny, b // (nx * ny))
                slot = 0
                for axis, i in steps_of(parts, share):
                    n = DIMS[parts][axis]
                    c = (coords[axis] - f) % n
                    slot = slot * 2 + ((c ^ (c >> 1)) >> i & 1)
                table[f, share, b] = slot
    return table


def partner_of(parts, me, f, axis, i):
    nx, ny, nz = DIMS[parts]
    coords = [me % nx, me // nx % ny, me // (nx * ny)]
    n = DIMS[parts][axis]
    block = 2 ** (i + 1)
    c = (coords[axis] - f + n) % n
    c = c - c % block + (block - 1 - c % block)
    coords[axis] = (c + f) % n
    return (coords[2] * ny + coords[1]) * nx + coords[0]


def swap_kernel(x_ref, wn_ref, ws_ref, xo_ref, wno_ref, wso_ref, send, recv):
    other = 1 - lax.axis_index("feat")
    barrier = pltpu.get_barrier_semaphore()
    pl.semaphore_signal(barrier, inc=1, device_id={"feat": other}, device_id_type=MESH)
    pl.semaphore_wait(barrier, 1)
    copies = []
    for k, (a, b) in enumerate(((x_ref, xo_ref), (wn_ref, wno_ref), (ws_ref, wso_ref))):
        copy = pltpu.make_async_remote_copy(
            src_ref=a,
            dst_ref=b,
            send_sem=send.at[k],
            recv_sem=recv.at[k],
            device_id={"feat": other},
            device_id_type=MESH,
        )
        copy.start()
        copies.append(copy)
    for copy in copies:
        copy.wait()


def swap(features, wn, ws):
    anywhere = pl.BlockSpec(memory_space=pl.ANY)
    return pl.pallas_call(
        swap_kernel,
        out_shape=[jax.ShapeDtypeStruct(a.shape, a.dtype) for a in (features, wn, ws)],
        in_specs=[anywhere] * 3,
        out_specs=[anywhere] * 3,
        scratch_shapes=[pltpu.SemaphoreType.DMA((3,)), pltpu.SemaphoreType.DMA((3,))],
        compiler_params=pltpu.CompilerParams(collective_id=0, has_side_effects=True),
        name="swap_halves",
    )(features, wn, ws)


def encode(load, count, rows, out, peak, inv):
    def largest(j, carry):
        v = jnp.abs(load(j))
        half = v.shape[1] // 2
        peak[pl.ds(j, 1), :] = jnp.max(jnp.maximum(v[:, :half], v[:, half:]), axis=0, keepdims=True)
        return carry

    lax.fori_loop(0, count, largest, 0, unroll=True)
    top = jnp.maximum(peak[:count, :], 1e-30)
    code = jnp.ceil(jnp.log2(top) * 256.0) + 1.0
    out[count * rows :, :] = code.astype(jnp.int32)
    inv[:count, :] = jnp.exp2(code * (-1.0 / 256.0)) * 32767.0

    def pack(j, carry):
        v = load(j)
        half = v.shape[1] // 2
        s = inv[pl.ds(j, 1), :]
        low = jnp.round(v[:, :half] * s).astype(jnp.int32)
        high = jnp.round(v[:, half:] * s).astype(jnp.int32)
        out[pl.ds(j * rows, rows), :] = jnp.bitwise_or(
            jnp.left_shift(high, 16), jnp.bitwise_and(low, 0xFFFF)
        )
        return carry

    lax.fori_loop(0, count, pack, 0, unroll=True)


def decode_add(src, total, rows, low, high, work, first, scale):
    count = high - low
    code = src[total * rows :, :].astype(jnp.float32)
    scale[:total, :] = jnp.exp2(code * (1.0 / 256.0)) * (1.0 / 32767.0)

    def add(j, carry):
        word = src[pl.ds((low + j) * rows, rows), :]
        s = scale[pl.ds(low + j, 1), :]
        a = jnp.right_shift(jnp.left_shift(word, 16), 16).astype(jnp.float32) * s
        b = jnp.right_shift(word, 16).astype(jnp.float32) * s
        half = a.shape[1]
        work[first + low + j, :, :half] += a
        work[first + low + j, :, half:] += b
        return carry

    lax.fori_loop(0, count, add, 0, unroll=True)


def first_layer_kernel(parts, *refs):
    (where, table, dst, src, limit, xa, xb, wa, wb, sa, sb, tiles) = refs[:12]
    keeps, messages, own_out = refs[12:15], refs[15:18], refs[18]
    accs, sends = refs[19:22], refs[22:25]
    order, count, gathered_a, gathered_b, peak, inv, sem = refs[25:]
    f, me = where[0], where[1]
    n_tiles, rows, size = tiles.shape
    blocks = xa.shape[0] // size
    half = parts // 2

    def clear(j, carry):
        for acc in accs:
            acc[j] = jnp.zeros(acc.shape[1:], jnp.float32)
        return carry

    lax.fori_loop(0, parts, clear, 0, unroll=4)
    for s in range(blocks):
        count[s] = 0

    def place(t, carry):
        s = src[t]
        at = count[s]
        order[s, at] = t
        count[s] = at + 1
        return carry

    lax.fori_loop(0, n_tiles, place, 0)

    mine = pl.ds(pl.multiple_of(f * rows, rows), rows)
    own_out[...] = jnp.dot(xa[mine, :], sa[...], preferred_element_type=jnp.float32) + jnp.dot(
        xb[mine, :], sb[...], preferred_element_type=jnp.float32
    )
    row_ids = lax.broadcasted_iota(jnp.int32, (rows, size), 0) + f * rows
    bases = [table[f, share, me] for share in range(len(SHARES))]

    def block(s, carry):
        n = count[s]
        at_source = pl.ds(pl.multiple_of(s * size, size), size)

        def group(g, inner):
            ids, parts_of = [], []
            for j in range(GROUP):
                k = g * GROUP + j
                valid = k < n
                t = jnp.where(valid, order[s, jnp.minimum(k, n_tiles - 1)], 0)
                ids.append(t)
                bound = jnp.where(valid, limit[t], 0)
                tile = tiles[t]
                parts_of.append(jnp.where(row_ids < bound, tile, jnp.zeros_like(tile)))
            a = jnp.concatenate(parts_of, axis=0)
            gathered_a[...] = jnp.dot(a, xa[at_source, :], preferred_element_type=jnp.float32).astype(
                jnp.bfloat16
            )
            gathered_b[...] = jnp.dot(a, xb[at_source, :], preferred_element_type=jnp.float32).astype(
                jnp.bfloat16
            )
            h = jnp.dot(gathered_a[...], wa[...], preferred_element_type=jnp.float32) + jnp.dot(
                gathered_b[...], wb[...], preferred_element_type=jnp.float32
            )
            for j in range(GROUP):
                d = dst[ids[j]]
                for share, (start, length) in enumerate(SHARES):
                    slot = jnp.bitwise_xor(table[f, share, d], bases[share])
                    at = j * rows + start
                    accs[share][slot] += h[at : at + length, :]
            return inner

        return lax.fori_loop(0, (n + GROUP - 1) // GROUP, group, carry)

    lax.fori_loop(0, blocks, block, 0)

    copies = []
    for share in range(len(SHARES)):
        copy = pltpu.make_async_copy(accs[share].at[pl.ds(0, half)], keeps[share], sem.at[share, 0])
        copy.start()
        copies.append(copy)
    chunk = chunk_of(parts)
    pieces = half // chunk
    for piece in range(pieces):
        for share, (start, length) in enumerate(SHARES):
            acc = accs[share]
            first = half + (pieces - 1 - piece) * chunk
            out = sends[share].at[piece]
            encode(lambda j: acc[first + j], chunk, length, out, peak, inv)
            copy = pltpu.make_async_copy(out, messages[share].at[piece], sem.at[share, 1 + piece])
            copy.start()
            copies.append(copy)
    for copy in copies:
        copy.wait()


def first_layer(parts, where, dst, src, limit, features, other, wn, wn_other, ws, ws_other, tiles):
    n_tiles, size, _ = tiles.shape
    rows = size // 2
    width = wn.shape[1]
    half = parts // 2
    chunk = chunk_of(parts)
    pieces = half // chunk
    anywhere = pl.BlockSpec(memory_space=pl.ANY)
    lengths = [length for _, length in SHARES]
    message = [(pieces, chunk * n + chunk, width // 2) for n in lengths]

    def fixed(shape):
        return pl.BlockSpec(shape, lambda i, where, *rest: (0,) * len(shape), pipeline_mode=pl.Buffered(1))

    grid_spec = pltpu.PrefetchScalarGridSpec(
        num_scalar_prefetch=5,
        grid=(1,),
        in_specs=[fixed(a.shape) for a in (features, other, wn, wn_other, ws, ws_other)]
        + [
            pl.BlockSpec(
                (n_tiles, rows, size), lambda i, where, *rest: (0, where[0], 0), pipeline_mode=pl.Buffered(1)
            )
        ],
        out_specs=[anywhere] * 6 + [fixed((rows, width))],
        scratch_shapes=[pltpu.VMEM((parts, n, width), jnp.float32) for n in lengths]
        + [pltpu.VMEM(shape, jnp.int32) for shape in message]
        + [
            pltpu.SMEM((features.shape[0] // size, n_tiles), jnp.int32),
            pltpu.SMEM((features.shape[0] // size,), jnp.int32),
            pltpu.VMEM((GROUP * rows, features.shape[1]), jnp.bfloat16),
            pltpu.VMEM((GROUP * rows, features.shape[1]), jnp.bfloat16),
            pltpu.VMEM((max(chunk, 8), width // 2), jnp.float32),
            pltpu.VMEM((max(chunk, 8), width // 2), jnp.float32),
            pltpu.SemaphoreType.DMA((len(SHARES), 1 + pieces)),
        ],
    )
    return pl.pallas_call(
        functools.partial(first_layer_kernel, parts),
        grid_spec=grid_spec,
        out_shape=[jax.ShapeDtypeStruct((half, n, width), jnp.float32) for n in lengths]
        + [jax.ShapeDtypeStruct(shape, jnp.int32) for shape in message]
        + [jax.ShapeDtypeStruct((rows, width), jnp.float32)],
        compiler_params=pltpu.CompilerParams(vmem_limit_bytes=VMEM_LIMIT),
        name="first_layer",
    )(
        where,
        jnp.asarray(slot_table(parts)),
        dst,
        src,
        limit,
        features,
        other,
        wn,
        wn_other,
        ws,
        ws_other,
        tiles,
    )


def message_plan(parts):
    plan = []
    count = parts // 2
    while count >= 1:
        size = min(count, chunk_of(parts))
        plan.append((count, size, count // size, count >= packed_from(parts)))
        count //= 2
    return plan


def second_layer_kernel(parts, *refs):
    nx, ny, nz = DIMS[parts]
    plane = nx * ny
    plan = message_plan(parts)
    n_shares = len(SHARES)
    keeps, messages = refs[0:3], refs[3:6]
    own_ref, list_ref, adj_ref, w_self_ref, w_neigh_ref, out_ref = refs[6:12]
    at = 12
    work = refs[at : at + 3]
    at += 3
    receive, outgoing = [], []
    for k in range(len(plan)):
        receive.append(refs[at : at + 3])
        at += 3
    for k in range(len(plan)):
        coded = plan[k][3] and k > 0
        outgoing.append(refs[at : at + 3] if coded else None)
        at += 3 if coded else 0
    (peak, inv, scale, onehot, hid_own, hid_other, rows_out, rows_mid, rows_next, rows_in, part, part_other) = refs[
        at : at + 12
    ]
    local_sem, send_sem, recv_sem, pair_sem, plane_sem, line_sem = refs[at + 12 :]

    f = lax.axis_index("feat")
    me = lax.axis_index("dom")
    z, q = me // plane, me % plane
    barrier = pltpu.get_barrier_semaphore()
    partners = [{"feat": 1 - f}]
    partners += [{"dom": z * plane + (q + d) % plane} for d in range(1, plane)]
    partners += [{"dom": (z + d) % nz * plane + q} for d in range(1, nz)]
    for partner in partners:
        pl.semaphore_signal(barrier, inc=1, device_id=partner, device_id_type=MESH)
    pl.semaphore_wait(barrier, len(partners))

    def message(k, share, piece, src):
        number = sum(p[2] for p in plan[:k]) + piece
        axis, i = steps_of(parts, share)[k]
        return pltpu.make_async_remote_copy(
            src_ref=src,
            dst_ref=receive[k][share].at[piece],
            send_sem=send_sem.at[share, number],
            recv_sem=recv_sem.at[share, number],
            device_id={"dom": partner_of(parts, me, f, axis, i)},
            device_id_type=MESH,
        )

    in_flight = {}
    for piece in range(plan[0][2]):
        for share in range(n_shares):
            copy = message(0, share, piece, messages[share].at[piece])
            copy.start()
            in_flight[0, share, piece] = copy
    loads = []
    for share in range(n_shares):
        copy = pltpu.make_async_copy(keeps[share], work[share], local_sem.at[share])
        copy.start()
        loads.append(copy)

    lanes = lax.broadcasted_iota(jnp.int32, onehot.shape[1:], 1)
    for b in range(onehot.shape[0]):
        ids = list_ref[pl.ds(b * onehot.shape[1], onehot.shape[1]), :]
        onehot[b] = jnp.where(ids == lanes, 1.0, 0.0).astype(jnp.bfloat16)
    for copy in loads:
        copy.wait()

    def absorb(k, share, piece, low, high):
        count, size, pieces, coded = plan[k]
        length = SHARES[share][1]
        first = (pieces - 1 - piece) * size
        if coded:
            decode_add(receive[k][share].at[piece], size, length, low, high, work[share], first, scale)
        else:
            for j in range(low, high):
                work[share][first + j] += receive[k][share][piece, j]

    def forward(k, share, piece):
        count, size, pieces, coded = plan[k]
        first = count + (pieces - 1 - piece) * size
        if coded:
            out = outgoing[k][share].at[piece]
            encode(lambda j: work[share][first + j], size, SHARES[share][1], out, peak, inv)
        else:
            out = work[share].at[pl.ds(first, size)]
        copy = message(k, share, piece, out)
        copy.start()
        in_flight[k, share, piece] = copy

    for k, (count, size, pieces, coded) in enumerate(plan):
        for piece in range(pieces):
            for share in range(n_shares):
                in_flight[k, share, piece].wait_recv()
                if pieces > 1:
                    absorb(k, share, piece, 0, size)
                    if piece < pieces // 2:
                        forward(k + 1, share, piece)
                elif k + 1 < len(plan):
                    absorb(k, share, piece, size // 2, size)
                    forward(k + 1, share, 0)
                    absorb(k, share, piece, 0, size // 2)
                else:
                    absorb(k, share, piece, 0, size)

    for share, (start, length) in enumerate(SHARES):
        total = work[share][0] + own_ref[start : start + length, :]
        work[share][0] = jnp.maximum(total, 0.0)
    hid_own[...] = jnp.concatenate([work[share][0] for share in range(n_shares)], axis=0).astype(jnp.bfloat16)

    def to_pair(src, dst, number):
        return pltpu.make_async_remote_copy(
            src_ref=src,
            dst_ref=dst,
            send_sem=pair_sem.at[0, number],
            recv_sem=pair_sem.at[1, number],
            device_id={"feat": 1 - f},
            device_id_type=MESH,
        )

    share_hidden = to_pair(hid_own, hid_other, 0)
    share_hidden.start()
    share_hidden.wait()
    width = hid_own.shape[1] // 2
    mine, theirs = hid_own[...], hid_other[...]
    own_half = jnp.where(f == 0, mine[:, :width], mine[:, width:])
    other_half = jnp.where(f == 0, theirs[:, :width], theirs[:, width:])
    low = jnp.where(f == 0, own_half, other_half)
    high = jnp.where(f == 0, other_half, own_half)
    hidden = jnp.concatenate([low, high], axis=0)
    per_plane = rows_out.shape[1]
    for b in range(plane):
        rows_out[b] = jnp.dot(onehot[b], hidden, preferred_element_type=jnp.float32).astype(jnp.bfloat16)

    plane_copies = []
    for d in range(1, plane):
        to = (q + d) % plane
        copy = pltpu.make_async_remote_copy(
            src_ref=rows_out.at[to],
            dst_ref=rows_mid.at[q],
            send_sem=plane_sem.at[0, d],
            recv_sem=plane_sem.at[1, d],
            device_id={"dom": z * plane + to},
            device_id_type=MESH,
        )
        copy.start()
        plane_copies.append(copy)
    rows_mid[q] = rows_out[q]
    for copy in plane_copies:
        copy.wait_recv()
    slots = per_plane // nz
    arrived = [rows_mid[s].astype(jnp.float32) for s in range(plane)]
    for r in range(nz):
        rows_next[r] = jnp.concatenate(
            [v[r * slots : (r + 1) * slots, :] for v in arrived], axis=0
        ).astype(jnp.bfloat16)
    line_copies = []
    for d in range(1, nz):
        to = (z + d) % nz
        copy = pltpu.make_async_remote_copy(
            src_ref=rows_next.at[to],
            dst_ref=rows_in.at[z],
            send_sem=line_sem.at[0, d],
            recv_sem=line_sem.at[1, d],
            device_id={"dom": to * plane + q},
            device_id_type=MESH,
        )
        copy.start()
        line_copies.append(copy)
    rows_in[z] = rows_next[z]
    half_rows = pl.ds(pl.multiple_of(f * width, width), width)
    n_own = hidden.shape[0]
    total = jnp.dot(adj_ref[:, :n_own], hidden, preferred_element_type=jnp.float32)
    logits = jnp.dot(hidden[: out_ref.shape[0]], w_self_ref[half_rows, :], preferred_element_type=jnp.float32)
    for copy in line_copies:
        copy.wait_recv()
    pool = jnp.concatenate([rows_in[s] for s in range(nz)], axis=0)
    total += jnp.dot(adj_ref[:, n_own:], pool, preferred_element_type=jnp.float32)
    logits += jnp.dot(total.astype(jnp.bfloat16), w_neigh_ref[half_rows, :], preferred_element_type=jnp.float32)
    part[...] = logits
    share_logits = to_pair(part, part_other, 1)
    share_logits.start()
    share_logits.wait()
    out_ref[...] = part[...] + part_other[...]
    for copy in plane_copies + line_copies:
        copy.wait_send()
    for copy in in_flight.values():
        copy.wait_send()


def second_layer(parts, keeps, messages, own, lists, adj, w_self, w_neigh):
    nx, ny, nz = DIMS[parts]
    plane = nx * ny
    plan = message_plan(parts)
    whole = pl.BlockSpec(memory_space=pltpu.VMEM)
    anywhere = pl.BlockSpec(memory_space=pl.ANY)
    rows, width = own.shape
    half = width // 2
    lengths = [length for _, length in SHARES]
    slots = lists.shape[0] // parts
    buffers = [pltpu.VMEM(a.shape, jnp.float32) for a in keeps]
    for count, size, pieces, coded in plan:
        for n in lengths:
            if coded:
                buffers.append(pltpu.VMEM((pieces, size * n + size, half), jnp.int32))
            else:
                buffers.append(pltpu.VMEM((pieces, size, n, width), jnp.float32))
    for k, (count, size, pieces, coded) in enumerate(plan):
        if coded and k > 0:
            buffers += [pltpu.VMEM((pieces, size * n + size, half), jnp.int32) for n in lengths]
    chunk = max(chunk_of(parts), 8)
    buffers += [pltpu.VMEM((chunk, half), jnp.float32)] * 3
    buffers += [
        pltpu.VMEM((plane, nz * slots, 2 * rows), jnp.bfloat16),
        pltpu.VMEM((rows, width), jnp.bfloat16),
        pltpu.VMEM((rows, width), jnp.bfloat16),
        pltpu.VMEM((plane, nz * slots, half), jnp.bfloat16),
        pltpu.VMEM((plane, nz * slots, half), jnp.bfloat16),
        pltpu.VMEM((nz, plane * slots, half), jnp.bfloat16),
        pltpu.VMEM((nz, plane * slots, half), jnp.bfloat16),
        pltpu.VMEM((adj.shape[0], w_self.shape[1]), jnp.float32),
        pltpu.VMEM((adj.shape[0], w_self.shape[1]), jnp.float32),
    ]
    numbers = sum(p[2] for p in plan)
    dma = pltpu.SemaphoreType.DMA
    buffers += [
        dma((len(SHARES),)),
        dma((len(SHARES), numbers)),
        dma((len(SHARES), numbers)),
        dma((2, 2)),
        dma((2, plane)),
        dma((2, nz)),
    ]
    return pl.pallas_call(
        functools.partial(second_layer_kernel, parts),
        out_shape=jax.ShapeDtypeStruct((adj.shape[0], w_self.shape[1]), jnp.float32),
        in_specs=[anywhere] * 6 + [whole] * 5,
        out_specs=whole,
        scratch_shapes=buffers,
        compiler_params=pltpu.CompilerParams(
            collective_id=1, has_side_effects=True, vmem_limit_bytes=VMEM_LIMIT
        ),
        name="reduce_and_second_layer",
    )(*keeps, *messages, own, lists, adj, w_self, w_neigh)


def body(
    features,
    tile_weight,
    tile_dst,
    tile_src,
    tile_rows,
    w_self1,
    neighbour_weight_first,
    send_list,
    send_count,
    adj_two,
    w_self2,
    w_neigh2,
):
    parts = lax.axis_size("dom")
    f, me = lax.axis_index("feat"), lax.axis_index("dom")
    nx, ny, nz = DIMS[parts]
    slots = send_list.shape[2]
    lists = lax.dynamic_index_in_dim(send_list, me, 0, keepdims=False)
    counts = lax.dynamic_index_in_dim(send_count, me, 0, keepdims=False)
    lists = jnp.where(jnp.arange(slots)[None, :] < counts[:, None], lists, -1)
    lists = lists.reshape(nz, nx * ny, slots).transpose(1, 0, 2).reshape(parts * slots, 1)
    where = jnp.stack([f, me]).astype(jnp.int32)

    other, wn_other, ws_other = swap(features, neighbour_weight_first, w_self1)
    results = first_layer(
        parts,
        where,
        tile_dst,
        tile_src,
        tile_rows,
        features,
        other,
        neighbour_weight_first,
        wn_other,
        w_self1,
        ws_other,
        tile_weight,
    )
    return second_layer(parts, results[:3], results[3:6], results[6], lists, adj_two, w_self2, w_neigh2)


def solution(mesh):
    in_specs = (
        P("dom", "feat"),
        P("dom", None, None),
        P("dom"),
        P("dom"),
        P("dom"),
        P("feat", None),
        P("feat", None),
        P(),
        P(),
        P("dom", None),
        P(),
        P(),
    )
    out_specs = P("dom", None)
    return jax.shard_map(body, mesh=mesh, in_specs=in_specs, out_specs=out_specs, check_vma=False)
```

time: 972 us -> 110 us (0.11)
  waiting for transfers between devices: 749 us -> 0 us
  Pallas kernels: 0 us -> 104 us
  blocking collectives: 99.9 us -> 0 us
  matrix products: 65.5 us -> 0 us
  local copies, waits for them, and re-layouts: 38.3 us -> 4.96 us
  between operations: 13.6 us -> 0.07 us
    reduce_scatter x1 -> x0, waiting for transfers between devices: 639 us -> none  [body(): lax.psum_scatter(summed.reshape(lax.axis_size('dom') * tile_size, hidden_...]
    all_gather x1 -> x0, waiting for transfers between devices: 110 us -> none  [pull_rows(): everything = lax.all_gather(hidden, 'dom', axis=0, tiled=True)]
    pallas_call x0 -> x3, Pallas kernels: none -> 104 us  [the longest x1 66.3 us: second_layer(): pl.pallas_call(functools.partial(second_layer_kernel, parts), out_shape=j...]
    psum x1 -> x0, blocking collectives: 99.9 us -> none  [body(): pre = lax.psum(total, 'feat')]
    dot_general x6 -> x0, matrix products: 65.5 us -> none  [the longest x1 30.1 us: body(): jnp.einsum('kys,sj->kyj', collected_rows, neighbour_weight_first, preferr...]
    dot_general x1 -> x0, local copies, waits for them, and re-layouts: 17.7 us -> none  [body(): jnp.einsum('tb,trh->brh', onehot, neighbour_rows, precision=lax.Precision...]
    gather x2 -> x0, local copies, waits for them, and re-layouts: 17.4 us -> none  [the longest x1 9.46 us: body(): source_nodes = jnp.take(blocks, tile_src, axis=0)]
  transfers between devices with their start and end apart: 2 -> 0, of which waited for: 2 -> 0; matrix products, arithmetic and copies ran while one was open for 0% -> 0% of each run, Pallas kernels for 0% -> 0%
where the time goes in v1:
time: 110 us
  Pallas kernels  104 us (95%)
  local copies, waits for them, and re-layouts  4.96 us (5%)
    pallas_call x1, Pallas kernels, second_layer(): pl.pallas_call(functools.partial(second_layer_kernel, parts), out_shape=j...  66.3 us
    pallas_call x1, Pallas kernels, first_layer(): pl.pallas_call(functools.partial(first_layer_kernel, parts), grid_spec=gr...  31.5 us
    pallas_call x1, Pallas kernels, swap(): pl.pallas_call(swap_kernel, out_shape=[jax.ShapeDtypeStruct(a.shape, a.dt...  6.67 us
    unnamed x9, local copies, waits for them, and re-layouts  3 us

profile of v1, /device:TPU:1, one launch (start us, length us, event | category | flops | bytes accessed | tf_op | source)
XLA Modules:
  0.0 110.1 jit_solution(3379718292771366821)
XLA Ops:
  0.0 0.0 copy-start
  0.0 0.6 pad_add_fusion.refs_0_
  0.6 6.7 %swap_halves.1 = (bf16[1024,512]{1,0:T(8,128)(2,1)}, bf16[512,256]{1,0:T(8,128)(2,1)}, bf16[512,256]{1,0:T(8,128)(2,1)}) custom-call(bf16[1024,512]{1,0:T(8,128)(2,1)} %refs_5_.1, bf16[512,256]{1,0:T(8,128)(2,1)} %refs_7_.1, bf16[512,256]{1,0:T(8,128)(2,1)} %refs_9_.2), custom_call_target="tpu_custom_call" | custom-call | tf_op jit(solution)/shard_map/swap_halves/pallas_call | solution.py:87
  7.3 0.0 copy-start.1
  7.3 0.0 copy-start.2
  7.3 31.5 %first_layer.1 = (f32[64,24,256]{2,1,0:T(8,128)}, f32[64,24,256]{2,1,0:T(8,128)}, f32[64,16,256]{2,1,0:T(8,128)}, s32[4,400,128]{2,1,0:T(8,128)}, s32[4,400,128]...) custom-call(s32[2]{0:T(128)} %pad_add_fusion.refs_0_, s32[2,3,128]{2,1,0:T(4,128)} %constant.23.clone.refs_1_, ...), custom_call_target="tpu_custom_call" | custom-call | tf_op jit(solution)/shard_map/first_layer/pallas_call | solution.py:270
  38.8 0.0 copy-done
  38.9 0.1 squeeze.6
  38.9 0.7 dynamic-slice_reduce_fusion
  39.6 0.1 lt.24
  39.7 0.1 copy.17
  39.8 1.0 reshape.16.refs_7_
  40.8 0.0 copy-done.1
  40.8 0.8 copy.19.refs_9_
  41.6 0.0 copy-done.2
  41.6 0.8 copy.20.refs_10_
  42.3 66.3 %reduce_and_second_layer.1 = f32[64,172]{1,0:T(8,128)} custom-call(f32[64,24,256]{2,1,0:T(8,128)} %get-tuple-element.18.refs_0_, f32[64,24,256]{2,1,0:T(8,128)} %get-tuple-element.19.refs_1_, f32[64,16,256]{2,1,0:T(8,128)} %get-tuple-element.20.refs_2_, s32[4,400,128]{2,1,0:T(8,128)} %get-tuple-element.21.refs_3_, s32[4,400,128]{2,1,0:T(8,128)} %get-tuple-element.22.refs_4_, ...), custom_call_target="tpu_custom_call" | custom-call | tf_op jit(solution)/shard_map/reduce_and_second_layer/pallas_call | solution.py:534
  108.6 1.5 %copy.22 = f32[64,172]{1,0:T(8,128)} copy(f32[64,172]{1,0:T(8,128)} %reduce_and_second_layer.1) | data formatting | bytes 88064
  (2 shorter events, 0.0 us)
Async XLA Ops:
  0.0 38.8 %copy-start = (s32[128,128,8]{1,2,0:T(8,128)S(1)}, s32[128,128,8]{1,2,0:T(8,128)}, u32[]{:S(2)}) copy-start(s32[128,128,8]{1,2,0:T(8,128)} %param.20) | copy-start | bytes 1572868
  7.3 33.5 %copy-start.1 = (bf16[256,172]{0,1:T(8,128)(2,1)S(1)}, bf16[256,172]{0,1:T(8,128)(2,1)}, u32[]{:S(2)}) copy-start(bf16[256,172]{0,1:T(8,128)(2,1)} %param.23) | copy-start | bytes 264196
  7.3 34.3 %copy-start.2 = (bf16[256,172]{0,1:T(8,128)(2,1)S(1)}, bf16[256,172]{0,1:T(8,128)(2,1)}, u32[]{:S(2)}) copy-start(bf16[256,172]{0,1:T(8,128)(2,1)} %param.24) | copy-start | bytes 264196

commit v2 on v1

v2 whole, which is shorter than its diff:
```python
import functools

import jax
import jax.numpy as jnp
import numpy as np
from jax import lax
from jax.experimental import pallas as pl
from jax.experimental.pallas import tpu as pltpu
from jax.sharding import PartitionSpec as P

DIMS = {128: (4, 4, 8), 16: (4, 2, 2)}
SHARES = ((0, 24), (24, 24), (48, 16))
ORDERS = ((0, 1, 2), (1, 0, 2), (2, 0, 1))
GROUP = 4
GROUPS = 2
VMEM_LIMIT = 56 * 1024 * 1024
MESH = pl.DeviceIdType.MESH


def bits_of(count):
    return count.bit_length() - 1


def steps_of(parts, share):
    dims = DIMS[parts]
    return [(axis, i) for axis in ORDERS[share] for i in range(bits_of(dims[axis]))]


def chunk_of(parts):
    return parts // 8


def packed_from(parts):
    return 8 if parts >= 128 else 2


@functools.lru_cache(maxsize=None)
def slot_table(parts):
    nx, ny, nz = DIMS[parts]
    table = np.zeros((2, len(SHARES), parts), np.int32)
    for f in range(2):
        for share in range(len(SHARES)):
            for b in range(parts):
                coords = (b % nx, b // nx % ny, b // (nx * ny))
                slot = 0
                for axis, i in steps_of(parts, share):
                    n = DIMS[parts][axis]
                    c = (coords[axis] - f) % n
                    slot = slot * 2 + ((c ^ (c >> 1)) >> i & 1)
                table[f, share, b] = slot
    return table


def place_of(parts, me):
    nx, ny, nz = DIMS[parts]
    return lax.rem(me, nx), lax.rem(lax.div(me, nx), ny), lax.div(me, nx * ny)


def partners_of(parts, me, f):
    nx, ny, nz = DIMS[parts]
    place = place_of(parts, me)
    pitch = (1, nx, nx * ny)
    found = {}
    for axis, n in enumerate(DIMS[parts]):
        c = lax.rem(place[axis] - f + n, n)
        for i in range(bits_of(n)):
            size = 2 ** (i + 1)
            at = lax.rem(c, size)
            other = lax.rem(c + (size - 1) - 2 * at + f, n)
            found[axis, i] = me + (other - place[axis]) * pitch[axis]
    return found


def swap_kernel(x_ref, wn_ref, ws_ref, xo_ref, wno_ref, wso_ref, send, recv):
    other = 1 - lax.axis_index("feat")
    barrier = pltpu.get_barrier_semaphore()
    pl.semaphore_signal(barrier, inc=1, device_id={"feat": other}, device_id_type=MESH)
    pl.semaphore_wait(barrier, 1)
    copies = []
    for k, (a, b) in enumerate(((x_ref, xo_ref), (wn_ref, wno_ref), (ws_ref, wso_ref))):
        copy = pltpu.make_async_remote_copy(
            src_ref=a,
            dst_ref=b,
            send_sem=send.at[k],
            recv_sem=recv.at[k],
            device_id={"feat": other},
            device_id_type=MESH,
        )
        copy.start()
        copies.append(copy)
    for copy in copies:
        copy.wait()


def swap(features, wn, ws):
    anywhere = pl.BlockSpec(memory_space=pl.ANY)
    return pl.pallas_call(
        swap_kernel,
        out_shape=[jax.ShapeDtypeStruct(a.shape, a.dtype) for a in (features, wn, ws)],
        in_specs=[anywhere] * 3,
        out_specs=[anywhere] * 3,
        scratch_shapes=[pltpu.SemaphoreType.DMA((3,)), pltpu.SemaphoreType.DMA((3,))],
        compiler_params=pltpu.CompilerParams(collective_id=0, has_side_effects=True),
        name="swap_halves",
    )(features, wn, ws)


def encode(load, count, rows, out, peak, inv):
    def largest(j, carry):
        v = jnp.abs(load(j))
        half = v.shape[1] // 2
        peak[pl.ds(j, 1), :] = jnp.max(jnp.maximum(v[:, :half], v[:, half:]), axis=0, keepdims=True)
        return carry

    lax.fori_loop(0, count, largest, 0, unroll=True)
    top = jnp.maximum(peak[:count, :], 1e-30)
    code = jnp.ceil(jnp.log2(top) * 256.0) + 1.0
    out[count * rows :, :] = code.astype(jnp.int32)
    inv[:count, :] = jnp.exp2(code * (-1.0 / 256.0)) * 32767.0

    def pack(j, carry):
        v = load(j)
        half = v.shape[1] // 2
        s = inv[pl.ds(j, 1), :]
        low = jnp.round(v[:, :half] * s).astype(jnp.int32)
        high = jnp.round(v[:, half:] * s).astype(jnp.int32)
        out[pl.ds(j * rows, rows), :] = jnp.bitwise_or(
            jnp.left_shift(high, 16), jnp.bitwise_and(low, 0xFFFF)
        )
        return carry

    lax.fori_loop(0, count, pack, 0, unroll=True)


def decode_add(src, total, rows, low, high, work, first, scale):
    count = high - low
    code = src[total * rows :, :].astype(jnp.float32)
    scale[:total, :] = jnp.exp2(code * (1.0 / 256.0)) * (1.0 / 32767.0)

    def add(j, carry):
        word = src[pl.ds((low + j) * rows, rows), :]
        s = scale[pl.ds(low + j, 1), :]
        a = jnp.right_shift(jnp.left_shift(word, 16), 16).astype(jnp.float32) * s
        b = jnp.right_shift(word, 16).astype(jnp.float32) * s
        half = a.shape[1]
        work[first + low + j, :, :half] += a
        work[first + low + j, :, half:] += b
        return carry

    lax.fori_loop(0, count, add, 0, unroll=True)


def first_layer_kernel(parts, *refs):
    table, dst, src, limit = refs[:4]
    inputs = refs[4:11]
    keeps, messages, own_out = refs[11:14], refs[14:17], refs[17]
    accs, sends = refs[18:21], refs[21:24]
    held = refs[24:31]
    order, count, plan, gathered, own, peak, inv, sem, load_sem = refs[31:]
    xa, xb, wa, wb, sa, sb, tiles = held
    f, me = lax.axis_index("feat"), lax.axis_index("dom")
    n_tiles, rows, size = tiles.shape
    blocks = xa.shape[0] // size
    half = parts // 2
    depth = xa.shape[1]
    group_rows = GROUP * rows

    loads = []
    for k in range(7):
        source = inputs[k].at[:, pl.ds(pl.multiple_of(f * rows, rows), rows), :] if k == 6 else inputs[k]
        copy = pltpu.make_async_copy(source, held[k], load_sem.at[k])
        copy.start()
        loads.append(copy)

    for s in range(blocks):
        count[s] = 0

    def place(t, carry):
        s = src[t]
        at = count[s]
        order[s, at] = t
        count[s] = at + 1
        return carry

    lax.fori_loop(0, n_tiles, place, 0)

    def groups_of(s, at):
        n = count[s]

        def one(g, at):
            plan[0, at] = s
            plan[1, at] = g * GROUP
            plan[2, at] = jnp.minimum(n - g * GROUP, GROUP)
            return at + 1

        return lax.fori_loop(0, lax.div(n + GROUP - 1, GROUP), one, at)

    n_groups = lax.fori_loop(0, blocks, groups_of, 0)
    for g in range(3 * GROUPS):
        plan[0, n_groups + g] = 0
        plan[1, n_groups + g] = 0
        plan[2, n_groups + g] = 0

    def clear(j, carry):
        for acc in accs:
            acc[j] = jnp.zeros(acc.shape[1:], jnp.float32)
        return carry

    lax.fori_loop(0, parts, clear, 0, unroll=4)
    for copy in loads:
        copy.wait()

    mine = pl.ds(pl.multiple_of(f * rows, rows), rows)
    own[...] = jnp.dot(xa[mine, :], sa[...], preferred_element_type=jnp.float32) + jnp.dot(
        xb[mine, :], sb[...], preferred_element_type=jnp.float32
    )
    own_copy = pltpu.make_async_copy(own, own_out, load_sem.at[7])
    own_copy.start()
    row_ids = lax.broadcasted_iota(jnp.int32, (rows, size), 0) + f * rows
    bases = [table[f, share, me] for share in range(len(SHARES))]

    def gather(g, buffer):
        for u in range(GROUPS):
            s, first, n = plan[0, g + u], plan[1, g + u], plan[2, g + u]
            pieces = []
            for j in range(GROUP):
                valid = j < n
                t = jnp.where(valid, order[s, first + j], 0)
                tile = tiles[t]
                pieces.append(jnp.where(row_ids < jnp.where(valid, limit[t], 0), tile, jnp.zeros_like(tile)))
            a = jnp.concatenate(pieces, axis=0)
            at_source = pl.ds(pl.multiple_of(s * size, size), size)
            at = slice(u * group_rows, (u + 1) * group_rows)
            buffer[at, :depth] = jnp.dot(a, xa[at_source, :], preferred_element_type=jnp.float32).astype(
                jnp.bfloat16
            )
            buffer[at, depth:] = jnp.dot(a, xb[at_source, :], preferred_element_type=jnp.float32).astype(
                jnp.bfloat16
            )

    def spread(g, buffer):
        h = jnp.dot(buffer[:, :depth], wa[...], preferred_element_type=jnp.float32) + jnp.dot(
            buffer[:, depth:], wb[...], preferred_element_type=jnp.float32
        )
        for u in range(GROUPS):
            s, first, n = plan[0, g + u], plan[1, g + u], plan[2, g + u]
            for j in range(GROUP):
                d = dst[jnp.where(j < n, order[s, first + j], 0)]
                for share, (start, length) in enumerate(SHARES):
                    slot = jnp.bitwise_xor(table[f, share, d], bases[share])
                    at = (u * GROUP + j) * rows + start
                    accs[share][slot] += h[at : at + length, :]

    gather(0, gathered.at[0])

    def step(i, carry):
        g = i * (2 * GROUPS)
        spread(g, gathered.at[0])
        gather(g + GROUPS, gathered.at[1])
        spread(g + GROUPS, gathered.at[1])
        gather(g + 2 * GROUPS, gathered.at[0])
        return carry

    lax.fori_loop(0, lax.div(n_groups + 2 * GROUPS - 1, 2 * GROUPS), step, 0)

    copies = [own_copy]
    for share in range(len(SHARES)):
        copy = pltpu.make_async_copy(accs[share].at[pl.ds(0, half)], keeps[share], sem.at[share, 0])
        copy.start()
        copies.append(copy)
    chunk = chunk_of(parts)
    pieces = half // chunk
    for piece in range(pieces):
        for share, (start, length) in enumerate(SHARES):
            acc = accs[share]
            first = half + (pieces - 1 - piece) * chunk
            out = sends[share].at[piece]
            encode(lambda j: acc[first + j], chunk, length, out, peak, inv)
            copy = pltpu.make_async_copy(out, messages[share].at[piece], sem.at[share, 1 + piece])
            copy.start()
            copies.append(copy)
    for copy in copies:
        copy.wait()


def first_layer(parts, dst, src, limit, features, other, wn, wn_other, ws, ws_other, tiles):
    n_tiles, size, _ = tiles.shape
    rows = size // 2
    width = wn.shape[1]
    half = parts // 2
    chunk = chunk_of(parts)
    pieces = half // chunk
    scalars = pl.BlockSpec(memory_space=pltpu.SMEM)
    anywhere = pl.BlockSpec(memory_space=pl.ANY)
    lengths = [length for _, length in SHARES]
    message = [(pieces, chunk * n + chunk, width // 2) for n in lengths]
    operands = (features, other, wn, wn_other, ws, ws_other)
    blocks = features.shape[0] // size
    return pl.pallas_call(
        functools.partial(first_layer_kernel, parts),
        in_specs=[scalars] * 4 + [anywhere] * 7,
        out_specs=[anywhere] * 7,
        scratch_shapes=[pltpu.VMEM((parts, n, width), jnp.float32) for n in lengths]
        + [pltpu.VMEM(shape, jnp.int32) for shape in message]
        + [pltpu.VMEM(a.shape, a.dtype) for a in operands]
        + [
            pltpu.VMEM((n_tiles, rows, size), tiles.dtype),
            pltpu.SMEM((blocks, n_tiles + GROUP), jnp.int32),
            pltpu.SMEM((blocks,), jnp.int32),
            pltpu.SMEM((3, n_tiles // GROUP + blocks + 3 * GROUPS), jnp.int32),
            pltpu.VMEM((2, GROUPS * GROUP * rows, 2 * features.shape[1]), jnp.bfloat16),
            pltpu.VMEM((rows, width), jnp.float32),
            pltpu.VMEM((max(chunk, 8), width // 2), jnp.float32),
            pltpu.VMEM((max(chunk, 8), width // 2), jnp.float32),
            pltpu.SemaphoreType.DMA((len(SHARES), 1 + pieces)),
            pltpu.SemaphoreType.DMA((8,)),
        ],
        out_shape=[jax.ShapeDtypeStruct((half, n, width), jnp.float32) for n in lengths]
        + [jax.ShapeDtypeStruct(shape, jnp.int32) for shape in message]
        + [jax.ShapeDtypeStruct((rows, width), jnp.float32)],
        compiler_params=pltpu.CompilerParams(vmem_limit_bytes=VMEM_LIMIT),
        name="first_layer",
    )(jnp.asarray(slot_table(parts)), dst, src, limit, *operands, tiles)


def message_plan(parts):
    plan = []
    count = parts // 2
    while count >= 1:
        size = min(count, chunk_of(parts))
        plan.append((count, size, count // size, count >= packed_from(parts)))
        count //= 2
    return plan


def second_layer_kernel(parts, *refs):
    nx, ny, nz = DIMS[parts]
    plane = nx * ny
    plan = message_plan(parts)
    n_shares = len(SHARES)
    keeps, messages = refs[0:3], refs[3:6]
    own_ref, list_ref, count_ref, adj_ref, w_self_ref, w_neigh_ref, out_ref = refs[6:13]
    at = 13
    work = refs[at : at + 3]
    at += 3
    receive, outgoing = [], []
    for k in range(len(plan)):
        receive.append(refs[at : at + 3])
        at += 3
    for k in range(len(plan)):
        coded = plan[k][3] and k > 0
        outgoing.append(refs[at : at + 3] if coded else None)
        at += 3 if coded else 0
    (peak, inv, scale, lists, onehot, hid_own, hid_other, rows_out, rows_in, part, part_other) = refs[at : at + 11]
    local_sem, send_sem, recv_sem, pair_sem, rows_sem = refs[at + 11 :]

    f = lax.axis_index("feat")
    me = lax.axis_index("dom")
    partners = partners_of(parts, me, f)
    rows_in[...] = jnp.zeros_like(rows_in)
    barrier = pltpu.get_barrier_semaphore()
    for target in [{"feat": 1 - f}] + [{"dom": dom} for dom in partners.values()]:
        pl.semaphore_signal(barrier, inc=1, device_id=target, device_id_type=MESH)
    pl.semaphore_wait(barrier, 1 + len(partners))

    def message(k, share, piece, src):
        number = sum(p[2] for p in plan[:k]) + piece
        return pltpu.make_async_remote_copy(
            src_ref=src,
            dst_ref=receive[k][share].at[piece],
            send_sem=send_sem.at[share, number],
            recv_sem=recv_sem.at[share, number],
            device_id={"dom": partners[steps_of(parts, share)[k]]},
            device_id_type=MESH,
        )

    in_flight = {}
    for piece in range(plan[0][2]):
        for share in range(n_shares):
            copy = message(0, share, piece, messages[share].at[piece])
            copy.start()
            in_flight[0, share, piece] = copy
    loads = []
    for share in range(n_shares):
        copy = pltpu.make_async_copy(keeps[share], work[share], local_sem.at[share])
        copy.start()
        loads.append(copy)

    get_lists = pltpu.make_async_copy(list_ref.at[me], lists, local_sem.at[len(SHARES)])
    get_lists.start()
    get_lists.wait()
    slots = lists.shape[0]
    shape = lists.shape
    lanes = lax.broadcasted_iota(jnp.int32, shape, 1)
    valid = lax.broadcasted_iota(jnp.int32, shape, 0) < count_ref[pl.ds(me, 1), :]
    wanted = jnp.where(valid, lists[...], -1).astype(jnp.float32)
    hidden_rows = onehot.shape[1]
    ids = lax.broadcasted_iota(jnp.int32, (slots, hidden_rows), 1).astype(jnp.float32)
    px, py, pz = place_of(parts, me)
    at_x = [lax.rem(px + d, nx) for d in range(nx)]
    at_y = [lax.rem(py + d, ny) * nx for d in range(ny)]
    at_z = [lax.rem(pz + d, nz) * (nx * ny) for d in range(nz)]
    receivers = []
    for d in range(nz // 2):
        by_parity = [jnp.where(f == odd, at_z[2 * d], at_z[2 * d + 1]) for odd in range(2)]
        for dy in range(ny):
            for dx in range(nx):
                receivers.append(at_x[dx] + at_y[dy] + by_parity[(dx + dy) % 2])

    for i in range(0, len(receivers), 2):
        pair = []
        for r in receivers[i : i + 2]:
            column = jnp.sum(jnp.where(lanes == r, wanted, 0.0), axis=1, keepdims=True)
            pair.append(jnp.where(column == ids, 1.0, 0.0))
        onehot[i * slots : (i + 2) * slots, :] = jnp.concatenate(pair, axis=0).astype(jnp.bfloat16)
    for copy in loads:
        copy.wait()

    def absorb(k, share, piece, low, high):
        count, size, pieces, coded = plan[k]
        length = SHARES[share][1]
        first = (pieces - 1 - piece) * size
        if coded:
            decode_add(receive[k][share].at[piece], size, length, low, high, work[share], first, scale)
        else:
            for j in range(low, high):
                work[share][first + j] += receive[k][share][piece, j]

    def forward(k, share, piece):
        count, size, pieces, coded = plan[k]
        first = count + (pieces - 1 - piece) * size
        if coded:
            out = outgoing[k][share].at[piece]
            encode(lambda j: work[share][first + j], size, SHARES[share][1], out, peak, inv)
        else:
            out = work[share].at[pl.ds(first, size)]
        copy = message(k, share, piece, out)
        copy.start()
        in_flight[k, share, piece] = copy

    for k, (count, size, pieces, coded) in enumerate(plan):
        for piece in range(pieces):
            for share in range(n_shares):
                in_flight[k, share, piece].wait_recv()
                if pieces > 1:
                    absorb(k, share, piece, 0, size)
                    if piece < pieces // 2:
                        forward(k + 1, share, piece)
                elif k + 1 < len(plan):
                    absorb(k, share, piece, size // 2, size)
                    forward(k + 1, share, 0)
                    absorb(k, share, piece, 0, size // 2)
                else:
                    absorb(k, share, piece, 0, size)

    for share, (start, length) in enumerate(SHARES):
        total = work[share][0] + own_ref[start : start + length, :]
        work[share][0] = jnp.maximum(total, 0.0)
    hid_own[...] = jnp.concatenate([work[share][0] for share in range(n_shares)], axis=0).astype(jnp.bfloat16)

    def to_pair(src, dst, number):
        return pltpu.make_async_remote_copy(
            src_ref=src,
            dst_ref=dst,
            send_sem=pair_sem.at[0, number],
            recv_sem=pair_sem.at[1, number],
            device_id={"feat": 1 - f},
            device_id_type=MESH,
        )

    share_hidden = to_pair(hid_own, hid_other, 0)
    share_hidden.start()
    share_hidden.wait()
    mine, theirs = hid_own[...], hid_other[...]
    hidden = jnp.concatenate([jnp.where(f == 0, mine, theirs), jnp.where(f == 0, theirs, mine)], axis=0)
    width = hidden.shape[1] // 2
    picked = jnp.dot(onehot[...], hidden, preferred_element_type=jnp.float32)
    for i in range(len(receivers)):
        block = picked[i * slots : (i + 1) * slots, :]
        rows_out[i] = jnp.concatenate([block[:, :width], block[:, width:]], axis=0).astype(jnp.bfloat16)

    def to_receiver(i):
        return pltpu.make_async_remote_copy(
            src_ref=rows_out.at[i],
            dst_ref=rows_in.at[me],
            send_sem=rows_sem.at[0],
            recv_sem=rows_sem.at[1],
            device_id={"dom": receivers[i]},
            device_id_type=MESH,
        )

    for i in range(1, len(receivers)):
        to_receiver(i).start()

    @pl.when(f == 0)
    def _():
        rows_in[me] = rows_out[0]

    @pl.when(f == 1)
    def _():
        to_receiver(0).start()

    n_own = hidden.shape[0]
    out_rows = out_ref.shape[0]
    own_total = jnp.dot(adj_ref[:, :n_own], hidden, preferred_element_type=jnp.float32)
    self_logits = lax.dot_general(
        hidden[:out_rows], w_self_ref[...], (((1,), (1,)), ((), ())), preferred_element_type=jnp.float32
    )
    blocks = len(receivers)

    def wait_rows(n):
        for number, ref in ((0, rows_out), (1, rows_in)):
            pltpu.make_async_copy(ref.at[pl.ds(0, n)], ref.at[pl.ds(0, n)], rows_sem.at[number]).wait()

    pl.when(f == 0)(lambda: wait_rows(blocks - 1))
    pl.when(f == 1)(lambda: wait_rows(blocks))

    arrived = rows_in[...].astype(jnp.float32)
    pool = [
        arrived[:, k * slots : (k + 1) * slots, :].reshape(parts * slots, width).astype(jnp.bfloat16)
        for k in range(2)
    ]
    for k in range(2):
        part[:, k * width : (k + 1) * width] = jnp.dot(
            adj_ref[:, n_own:], pool[k], preferred_element_type=jnp.float32
        )
    share_part = to_pair(part, part_other, 1)
    share_part.start()
    share_part.wait()
    aggregate = (part[...] + part_other[...] + own_total).astype(jnp.bfloat16)
    out_ref[...] = self_logits + lax.dot_general(
        aggregate, w_neigh_ref[...], (((1,), (1,)), ((), ())), preferred_element_type=jnp.float32
    )
    for copy in in_flight.values():
        copy.wait_send()


def second_layer(parts, keeps, messages, own, lists, counts, adj, w_self, w_neigh):
    plan = message_plan(parts)
    whole = pl.BlockSpec(memory_space=pltpu.VMEM)
    anywhere = pl.BlockSpec(memory_space=pl.ANY)
    rows, width = own.shape
    half = width // 2
    lengths = [length for _, length in SHARES]
    slots = lists.shape[1]
    buffers = [pltpu.VMEM(a.shape, jnp.float32) for a in keeps]
    for count, size, pieces, coded in plan:
        for n in lengths:
            if coded:
                buffers.append(pltpu.VMEM((pieces, size * n + size, half), jnp.int32))
            else:
                buffers.append(pltpu.VMEM((pieces, size, n, width), jnp.float32))
    for k, (count, size, pieces, coded) in enumerate(plan):
        if coded and k > 0:
            buffers += [pltpu.VMEM((pieces, size * n + size, half), jnp.int32) for n in lengths]
    chunk = max(chunk_of(parts), 8)
    buffers += [pltpu.VMEM((chunk, half), jnp.float32)] * 3
    buffers += [
        pltpu.VMEM(lists.shape[1:], jnp.int32),
        pltpu.VMEM((parts // 2 * slots, 2 * rows), jnp.bfloat16),
        pltpu.VMEM((rows, width), jnp.bfloat16),
        pltpu.VMEM((rows, width), jnp.bfloat16),
        pltpu.VMEM((parts // 2, 2 * slots, half), jnp.bfloat16),
        pltpu.VMEM((parts, 2 * slots, half), jnp.bfloat16),
        pltpu.VMEM((adj.shape[0], width), jnp.float32),
        pltpu.VMEM((adj.shape[0], width), jnp.float32),
    ]
    numbers = sum(p[2] for p in plan)
    dma = pltpu.SemaphoreType.DMA
    buffers += [
        dma((len(SHARES) + 1,)),
        dma((len(SHARES), numbers)),
        dma((len(SHARES), numbers)),
        dma((2, 2)),
        dma((2,)),
    ]
    return pl.pallas_call(
        functools.partial(second_layer_kernel, parts),
        out_shape=jax.ShapeDtypeStruct((adj.shape[0], w_self.shape[0]), jnp.float32),
        in_specs=[anywhere] * 6 + [whole, anywhere] + [whole] * 4,
        out_specs=whole,
        scratch_shapes=buffers,
        compiler_params=pltpu.CompilerParams(
            collective_id=1, has_side_effects=True, vmem_limit_bytes=VMEM_LIMIT
        ),
        name="reduce_and_second_layer",
    )(*keeps, *messages, own, lists, counts, adj, w_self, w_neigh)


def body(
    features,
    tile_weight,
    tile_dst,
    tile_src,
    tile_rows,
    w_self1,
    neighbour_weight_first,
    send_list,
    send_count,
    adj_two,
    w_self2,
    w_neigh2,
):
    parts = lax.axis_size("dom")
    other, wn_other, ws_other = swap(features, neighbour_weight_first, w_self1)
    results = first_layer(
        parts,
        tile_dst,
        tile_src,
        tile_rows,
        features,
        other,
        neighbour_weight_first,
        wn_other,
        w_self1,
        ws_other,
        tile_weight,
    )
    return second_layer(parts, results[:3], results[3:6], results[6], send_list.transpose(0, 2, 1), send_count, adj_two, w_self2.T, w_neigh2.T)


def solution(mesh):
    in_specs = (
        P("dom", "feat"),
        P("dom", None, None),
        P("dom"),
        P("dom"),
        P("dom"),
        P("feat", None),
        P("feat", None),
        P(),
        P(),
        P("dom", None),
        P(),
        P(),
    )
    out_specs = P("dom", None)
    return jax.shard_map(body, mesh=mesh, in_specs=in_specs, out_specs=out_specs, check_vma=False)
```

time: 110 us -> 90 us (0.82)
  Pallas kernels: 104 us -> 88.3 us
  local copies, waits for them, and re-layouts: 4.96 us -> 1.47 us
    pallas_call x1, Pallas kernels: 31.5 us -> 18.6 us  [first_layer(): pl.pallas_call(functools.partial(first_layer_kernel, parts), in_specs=[sc...]
    pallas_call x1, Pallas kernels: 66.3 us -> 63.1 us  [second_layer(): pl.pallas_call(functools.partial(second_layer_kernel, parts), out_shape=j...]
    unnamed x9 -> x1, local copies, waits for them, and re-layouts: 3 us -> 1.47 us
where the time goes in v2:
time: 90 us; the launch traced here: 89.8 us
  Pallas kernels  88.3 us (98%)
  local copies, waits for them, and re-layouts  1.47 us (2%)
    pallas_call x1, Pallas kernels, second_layer(): pl.pallas_call(functools.partial(second_layer_kernel, parts), out_shape=j...  63.1 us
    pallas_call x1, Pallas kernels, first_layer(): pl.pallas_call(functools.partial(first_layer_kernel, parts), in_specs=[sc...  18.6 us
    pallas_call x1, Pallas kernels, swap(): pl.pallas_call(swap_kernel, out_shape=[jax.ShapeDtypeStruct(a.shape, a.dt...  6.67 us

profile of v2, /device:TPU:1, one launch (start us, length us, event | category | flops | bytes accessed | tf_op | source)
XLA Modules:
  0.0 89.8 jit_solution(7969646237884724333)
XLA Ops:
  0.0 6.7 %swap_halves.1 = (bf16[1024,512]{1,0:T(8,128)(2,1)}, bf16[512,256]{1,0:T(8,128)(2,1)}, bf16[512,256]{1,0:T(8,128)(2,1)}) custom-call(bf16[1024,512]{1,0:T(8,128)(2,1)} %refs_4_.1, bf16[512,256]{1,0:T(8,128)(2,1)} %refs_6_.1, bf16[512,256]{1,0:T(8,128)(2,1)} %refs_8_.2), custom_call_target="tpu_custom_call" | custom-call | tf_op jit(solution)/shard_map/swap_halves/pallas_call | solution.py:97
  6.7 18.6 %first_layer.1 = (f32[64,24,256]{2,1,0:T(8,128)}, f32[64,24,256]{2,1,0:T(8,128)}, f32[64,16,256]{2,1,0:T(8,128)}, s32[4,400,128]{2,1,0:T(8,128)}, s32[4,400,128]...) custom-call(s32[2,3,128]{2,1,0:T(4,128)} %constant.2.clone.refs_0_, s32[128]{0:T(128)} %refs_1_.1, ...), custom_call_target="tpu_custom_call" | custom-call | tf_op jit(solution)/shard_map/first_layer/pallas_call | solution.py:299
  25.2 63.1 %reduce_and_second_layer.1 = f32[64,172]{1,0:T(8,128)} custom-call(f32[64,24,256]{2,1,0:T(8,128)} %get-tuple-element.18.refs_0_, f32[64,24,256]{2,1,0:T(8,128)} %get-tuple-element.19.refs_1_, f32[64,16,256]{2,1,0:T(8,128)} %get-tuple-element.20.refs_2_, s32[4,400,128]{2,1,0:T(8,128)} %get-tuple-element.21.refs_3_, s32[4,400,128]{2,1,0:T(8,128)} %get-tuple-element.22.refs_4_, ...), custom_call_target="tpu_custom_call" | custom-call | tf_op jit(solution)/shard_map/reduce_and_second_layer/pallas_call | solution.py:577
  88.3 1.5 %copy.15 = f32[64,172]{1,0:T(8,128)} copy(f32[64,172]{1,0:T(8,128)} %reduce_and_second_layer.1) | data formatting | bytes 88064

commit v3 on v2

--- a/solution.py
+++ b/solution.py
@@ -10,7 +10,18 @@
 
 DIMS = {128: (4, 4, 8), 16: (4, 2, 2)}
 SHARES = ((0, 24), (24, 24), (48, 16))
-ORDERS = ((0, 1, 2), (1, 0, 2), (2, 0, 1))
+
+
+def stages_of(parts, share):
+    bits = [[(axis, i) for i in range(bits_of(n))] for axis, n in enumerate(DIMS[parts])]
+    x, y, z = bits
+    if share == 0:
+        return [x[:1], x[1:], y, z]
+    if share == 1:
+        return [y[:1], y[1:], x, z] if len(y) > 1 else [y, x[:1], x[1:], z]
+    return [z[:1], z[1:2], z[2:] + x, y] if len(z) > 1 else [z, x[:1], x[1:], y]
+
+
 GROUP = 4
 GROUPS = 2
 VMEM_LIMIT = 56 * 1024 * 1024
@@ -22,16 +33,22 @@
 
 
 def steps_of(parts, share):
-    dims = DIMS[parts]
-    return [(axis, i) for axis in ORDERS[share] for i in range(bits_of(dims[axis]))]
+    return [bit for stage in stages_of(parts, share) for bit in stage]
 
 
 def chunk_of(parts):
     return parts // 8
 
 
-def packed_from(parts):
-    return 8 if parts >= 128 else 2
+def plan_of(parts, share):
+    plan = []
+    count = parts
+    for bits in stages_of(parts, share):
+        stay = count >> len(bits)
+        size = min(stay, chunk_of(parts))
+        plan.append((bits, stay, stay // size, size))
+        count = stay
+    return plan
 
 
 @functools.lru_cache(maxsize=None)
@@ -56,19 +73,21 @@
     return lax.rem(me, nx), lax.rem(lax.div(me, nx), ny), lax.div(me, nx * ny)
 
 
-def partners_of(parts, me, f):
+def chip_across(parts, me, f, bits):
     nx, ny, nz = DIMS[parts]
     place = place_of(parts, me)
     pitch = (1, nx, nx * ny)
-    found = {}
+    dom = me
     for axis, n in enumerate(DIMS[parts]):
+        flips = sorted(i for a, i in bits if a == axis)
+        if not flips:
+            continue
         c = lax.rem(place[axis] - f + n, n)
-        for i in range(bits_of(n)):
+        for i in flips:
             size = 2 ** (i + 1)
-            at = lax.rem(c, size)
-            other = lax.rem(c + (size - 1) - 2 * at + f, n)
-            found[axis, i] = me + (other - place[axis]) * pitch[axis]
-    return found
+            c = c + (size - 1) - 2 * lax.rem(c, size)
+        dom = dom + (lax.rem(c + f, n) - place[axis]) * pitch[axis]
+    return dom
 
 
 def swap_kernel(x_ref, wn_ref, ws_ref, xo_ref, wno_ref, wso_ref, send, recv):
@@ -115,7 +134,7 @@
     lax.fori_loop(0, count, largest, 0, unroll=True)
     top = jnp.maximum(peak[:count, :], 1e-30)
     code = jnp.ceil(jnp.log2(top) * 256.0) + 1.0
-    out[count * rows :, :] = code.astype(jnp.int32)
+    out[count * rows : count * rows + count, :] = code.astype(jnp.int32)
     inv[:count, :] = jnp.exp2(code * (-1.0 / 256.0)) * 32767.0
 
     def pack(j, carry):
@@ -134,7 +153,7 @@
 
 def decode_add(src, total, rows, low, high, work, first, scale):
     count = high - low
-    code = src[total * rows :, :].astype(jnp.float32)
+    code = src[total * rows : total * rows + total, :].astype(jnp.float32)
     scale[:total, :] = jnp.exp2(code * (1.0 / 256.0)) * (1.0 / 32767.0)
 
     def add(j, carry):
@@ -323,63 +342,62 @@
     )(jnp.asarray(slot_table(parts)), dst, src, limit, *operands, tiles)
 
 
-def message_plan(parts):
-    plan = []
-    count = parts // 2
-    while count >= 1:
-        size = min(count, chunk_of(parts))
-        plan.append((count, size, count // size, count >= packed_from(parts)))
-        count //= 2
-    return plan
-
-
 def second_layer_kernel(parts, *refs):
     nx, ny, nz = DIMS[parts]
     plane = nx * ny
-    plan = message_plan(parts)
     n_shares = len(SHARES)
+    plans = [plan_of(parts, share) for share in range(n_shares)]
+    n_stages = len(plans[0])
     keeps, messages = refs[0:3], refs[3:6]
     own_ref, list_ref, count_ref, adj_ref, w_self_ref, w_neigh_ref, out_ref = refs[6:13]
     at = 13
     work = refs[at : at + 3]
     at += 3
     receive, outgoing = [], []
-    for k in range(len(plan)):
+    for k in range(n_stages):
         receive.append(refs[at : at + 3])
         at += 3
-    for k in range(len(plan)):
-        coded = plan[k][3] and k > 0
-        outgoing.append(refs[at : at + 3] if coded else None)
-        at += 3 if coded else 0
+    for k in range(n_stages):
+        outgoing.append(refs[at : at + 3] if k > 0 else None)
+        at += 3 if k > 0 else 0
     (peak, inv, scale, lists, onehot, hid_own, hid_other, rows_out, rows_in, part, part_other) = refs[at : at + 11]
     local_sem, send_sem, recv_sem, pair_sem, rows_sem = refs[at + 11 :]
 
     f = lax.axis_index("feat")
     me = lax.axis_index("dom")
-    partners = partners_of(parts, me, f)
+    partners = {}
+    for share in range(n_shares):
+        for k, (bits, stay, pieces, size) in enumerate(plans[share]):
+            for mask in range(1, 2 ** len(bits)):
+                chosen = tuple(sorted(b for i, b in enumerate(bits) if mask >> (len(bits) - 1 - i) & 1))
+                if chosen not in partners:
+                    partners[chosen] = chip_across(parts, me, f, chosen)
     rows_in[...] = jnp.zeros_like(rows_in)
     barrier = pltpu.get_barrier_semaphore()
     for target in [{"feat": 1 - f}] + [{"dom": dom} for dom in partners.values()]:
         pl.semaphore_signal(barrier, inc=1, device_id=target, device_id_type=MESH)
     pl.semaphore_wait(barrier, 1 + len(partners))
 
-    def message(k, share, piece, src):
-        number = sum(p[2] for p in plan[:k]) + piece
+    def message(k, share, mask, piece, src):
+        bits, stay, pieces, size = plans[share][k]
+        index = (mask - 1) * pieces + piece
+        number = sum((2 ** len(p[0]) - 1) * p[2] for p in plans[share][:k]) + index
+        chosen = tuple(sorted(b for i, b in enumerate(bits) if mask >> (len(bits) - 1 - i) & 1))
         return pltpu.make_async_remote_copy(
             src_ref=src,
-            dst_ref=receive[k][share].at[piece],
+            dst_ref=receive[k][share].at[index],
             send_sem=send_sem.at[share, number],
             recv_sem=recv_sem.at[share, number],
-            device_id={"dom": partners[steps_of(parts, share)[k]]},
+            device_id={"dom": partners[chosen]},
             device_id_type=MESH,
         )
 
     in_flight = {}
-    for piece in range(plan[0][2]):
+    for piece in range(plans[0][0][2]):
         for share in range(n_shares):
-            copy = message(0, share, piece, messages[share].at[piece])
+            copy = message(0, share, 1, piece, messages[share].at[piece])
             copy.start()
-            in_flight[0, share, piece] = copy
+            in_flight[0, share, 1, piece] = copy
     loads = []
     for share in range(n_shares):
         copy = pltpu.make_async_copy(keeps[share], work[share], local_sem.at[share])
@@ -416,42 +434,46 @@
     for copy in loads:
         copy.wait()
 
-    def absorb(k, share, piece, low, high):
-        count, size, pieces, coded = plan[k]
-        length = SHARES[share][1]
+    def absorb(k, share, mask, piece, low, high):
+        bits, stay, pieces, size = plans[share][k]
         first = (pieces - 1 - piece) * size
-        if coded:
-            decode_add(receive[k][share].at[piece], size, length, low, high, work[share], first, scale)
-        else:
-            for j in range(low, high):
-                work[share][first + j] += receive[k][share][piece, j]
-
-    def forward(k, share, piece):
-        count, size, pieces, coded = plan[k]
-        first = count + (pieces - 1 - piece) * size
-        if coded:
-            out = outgoing[k][share].at[piece]
-            encode(lambda j: work[share][first + j], size, SHARES[share][1], out, peak, inv)
-        else:
-            out = work[share].at[pl.ds(first, size)]
-        copy = message(k, share, piece, out)
+        source = receive[k][share].at[(mask - 1) * pieces + piece]
+        decode_add(source, size, SHARES[share][1], low - first, high - first, work[share], first, scale)
+
+    def forward(k, share, mask, piece):
+        bits, stay, pieces, size = plans[share][k]
+        first = mask * stay + (pieces - 1 - piece) * size
+        out = outgoing[k][share].at[(mask - 1) * pieces + piece]
+        encode(lambda j: work[share][first + j], size, SHARES[share][1], out, peak, inv)
+        copy = message(k, share, mask, piece, out)
         copy.start()
-        in_flight[k, share, piece] = copy
-
-    for k, (count, size, pieces, coded) in enumerate(plan):
-        for piece in range(pieces):
-            for share in range(n_shares):
-                in_flight[k, share, piece].wait_recv()
-                if pieces > 1:
-                    absorb(k, share, piece, 0, size)
-                    if piece < pieces // 2:
-                        forward(k + 1, share, piece)
-                elif k + 1 < len(plan):
-                    absorb(k, share, piece, size // 2, size)
-                    forward(k + 1, share, 0)
-                    absorb(k, share, piece, 0, size // 2)
-                else:
-                    absorb(k, share, piece, 0, size)
+        in_flight[k, share, mask, piece] = copy
+
+    for k in range(n_stages):
+        for piece in range(plans[0][k][2]):
+            for share in reversed(range(n_shares)):
+                bits, stay, pieces, size = plans[share][k]
+                masks = range(1, 2 ** len(bits))
+                for mask in masks:
+                    in_flight[k, share, mask, piece].wait_recv()
+                top = (pieces - piece) * size
+                bottom = top - size
+                leaving = []
+                if k + 1 < n_stages:
+                    next_bits, next_stay, next_pieces, next_size = plans[share][k + 1]
+                    for mask in reversed(range(1, 2 ** len(next_bits))):
+                        for next_piece in range(next_pieces):
+                            low = mask * next_stay + (next_pieces - 1 - next_piece) * next_size
+                            if bottom <= low < top:
+                                leaving.append((low, low + next_size, mask, next_piece))
+                for low, high, mask, next_piece in leaving:
+                    for m in masks:
+                        absorb(k, share, m, piece, low, high)
+                    forward(k + 1, share, mask, next_piece)
+                rest = min([low for low, *_ in leaving] + [top])
+                if rest > bottom:
+                    for m in masks:
+                        absorb(k, share, m, piece, bottom, rest)
 
     for share, (start, length) in enumerate(SHARES):
         total = work[share][0] + own_ref[start : start + length, :]
@@ -536,7 +558,8 @@
 
 
 def second_layer(parts, keeps, messages, own, lists, counts, adj, w_self, w_neigh):
-    plan = message_plan(parts)
+    plans = [plan_of(parts, share) for share in range(len(SHARES))]
+    n_stages = len(plans[0])
     whole = pl.BlockSpec(memory_space=pltpu.VMEM)
     anywhere = pl.BlockSpec(memory_space=pl.ANY)
     rows, width = own.shape
@@ -544,15 +567,11 @@
     lengths = [length for _, length in SHARES]
     slots = lists.shape[1]
     buffers = [pltpu.VMEM(a.shape, jnp.float32) for a in keeps]
-    for count, size, pieces, coded in plan:
-        for n in lengths:
-            if coded:
-                buffers.append(pltpu.VMEM((pieces, size * n + size, half), jnp.int32))
-            else:
-                buffers.append(pltpu.VMEM((pieces, size, n, width), jnp.float32))
-    for k, (count, size, pieces, coded) in enumerate(plan):
-        if coded and k > 0:
-            buffers += [pltpu.VMEM((pieces, size * n + size, half), jnp.int32) for n in lengths]
+    for first_stage in (0, 1):
+        for k in range(first_stage, n_stages):
+            for share, n in enumerate(lengths):
+                bits, stay, pieces, size = plans[share][k]
+                buffers.append(pltpu.VMEM(((2 ** len(bits) - 1) * pieces, size * n + size, half), jnp.int32))
     chunk = max(chunk_of(parts), 8)
     buffers += [pltpu.VMEM((chunk, half), jnp.float32)] * 3
     buffers += [
@@ -565,7 +584,7 @@
         pltpu.VMEM((adj.shape[0], width), jnp.float32),
         pltpu.VMEM((adj.shape[0], width), jnp.float32),
     ]
-    numbers = sum(p[2] for p in plan)
+    numbers = max(sum((2 ** len(p[0]) - 1) * p[2] for p in plan) for plan in plans)
     dma = pltpu.SemaphoreType.DMA
     buffers += [
         dma((len(SHARES) + 1,)),

time: 90 us -> 85.4 us (0.949)
  Pallas kernels: 88.3 us -> 83.7 us
    pallas_call x1, Pallas kernels: 63.1 us -> 58.4 us  [second_layer(): pl.pallas_call(functools.partial(second_layer_kernel, parts), out_shape=j...]
where the time goes in v3:
time: 85.4 us; the launch traced here: 85.2 us
  Pallas kernels  83.7 us (98%)
  local copies, waits for them, and re-layouts  1.47 us (2%)
    pallas_call x1, Pallas kernels, second_layer(): pl.pallas_call(functools.partial(second_layer_kernel, parts), out_shape=j...  58.4 us
    pallas_call x1, Pallas kernels, first_layer(): pl.pallas_call(functools.partial(first_layer_kernel, parts), in_specs=[sc...  18.6 us
    pallas_call x1, Pallas kernels, swap(): pl.pallas_call(swap_kernel, out_shape=[jax.ShapeDtypeStruct(a.shape, a.dt...  6.67 us

profile of v3, /device:TPU:1, one launch (start us, length us, event | category | flops | bytes accessed | tf_op | source)
XLA Modules:
  0.0 85.2 jit_solution(13628494893285873917)
XLA Ops:
  0.0 6.7 %swap_halves.1 = (bf16[1024,512]{1,0:T(8,128)(2,1)}, bf16[512,256]{1,0:T(8,128)(2,1)}, bf16[512,256]{1,0:T(8,128)(2,1)}) custom-call(bf16[1024,512]{1,0:T(8,128)(2,1)} %refs_4_.1, bf16[512,256]{1,0:T(8,128)(2,1)} %refs_6_.1, bf16[512,256]{1,0:T(8,128)(2,1)} %refs_8_.2), custom_call_target="tpu_custom_call" | custom-call | tf_op jit(solution)/shard_map/swap_halves/pallas_call | solution.py:116
  6.7 18.6 %first_layer.1 = (f32[64,24,256]{2,1,0:T(8,128)}, f32[64,24,256]{2,1,0:T(8,128)}, f32[64,16,256]{2,1,0:T(8,128)}, s32[4,400,128]{2,1,0:T(8,128)}, s32[4,400,128]...) custom-call(s32[2,3,128]{2,1,0:T(4,128)} %constant.2.clone.refs_0_, s32[128]{0:T(128)} %refs_1_.1, ...), custom_call_target="tpu_custom_call" | custom-call | tf_op jit(solution)/shard_map/first_layer/pallas_call | solution.py:318
  25.3 58.4 %reduce_and_second_layer.1 = f32[64,172]{1,0:T(8,128)} custom-call(f32[64,24,256]{2,1,0:T(8,128)} %get-tuple-element.18.refs_0_, f32[64,24,256]{2,1,0:T(8,128)} %get-tuple-element.19.refs_1_, f32[64,16,256]{2,1,0:T(8,128)} %get-tuple-element.20.refs_2_, s32[4,400,128]{2,1,0:T(8,128)} %get-tuple-element.21.refs_3_, s32[4,400,128]{2,1,0:T(8,128)} %get-tuple-element.22.refs_4_, ...), custom_call_target="tpu_custom_call" | custom-call | tf_op jit(solution)/shard_map/reduce_and_second_layer/pallas_call | solution.py:596
  83.7 1.5 %copy.15 = f32[64,172]{1,0:T(8,128)} copy(f32[64,172]{1,0:T(8,128)} %reduce_and_second_layer.1) | data formatting | bytes 88064

commit v4 on v3

--- a/solution.py
+++ b/solution.py
@@ -16,15 +16,16 @@
     bits = [[(axis, i) for i in range(bits_of(n))] for axis, n in enumerate(DIMS[parts])]
     x, y, z = bits
     if share == 0:
-        return [x[:1], x[1:], y, z]
+        return [x[:1], x[1:], y + z[:1], z[1:]] if len(z) > 1 else [x[:1], x[1:], y, z]
     if share == 1:
-        return [y[:1], y[1:], x, z] if len(y) > 1 else [y, x[:1], x[1:], z]
-    return [z[:1], z[1:2], z[2:] + x, y] if len(z) > 1 else [z, x[:1], x[1:], y]
+        return [y[:1], y[1:], x + z[:1], z[1:]] if len(y) > 1 else [y, x[:1], x[1:], z]
+    return [z[:1], z[1:2], x[:1] + y[:1], x[1:] + y[1:] + z[2:]] if len(z) > 1 else [z, x[:1], x[1:], y]
 
 
 GROUP = 4
 GROUPS = 2
-VMEM_LIMIT = 56 * 1024 * 1024
+FIRST_VMEM = 52 * 1024 * 1024
+SECOND_VMEM = 32 * 1024 * 1024
 MESH = pl.DeviceIdType.MESH
 
 
@@ -172,10 +173,9 @@
 def first_layer_kernel(parts, *refs):
     table, dst, src, limit = refs[:4]
     inputs = refs[4:11]
-    keeps, messages, own_out = refs[11:14], refs[14:17], refs[17]
-    accs, sends = refs[18:21], refs[21:24]
-    held = refs[24:31]
-    order, count, plan, gathered, own, peak, inv, sem, load_sem = refs[31:]
+    accs, sends, own = refs[11:14], refs[14:17], refs[17]
+    held = refs[18:25]
+    order, count, plan, gathered, peak, inv, load_sem = refs[25:]
     xa, xb, wa, wb, sa, sb, tiles = held
     f, me = lax.axis_index("feat"), lax.axis_index("dom")
     n_tiles, rows, size = tiles.shape
@@ -233,8 +233,6 @@
     own[...] = jnp.dot(xa[mine, :], sa[...], preferred_element_type=jnp.float32) + jnp.dot(
         xb[mine, :], sb[...], preferred_element_type=jnp.float32
     )
-    own_copy = pltpu.make_async_copy(own, own_out, load_sem.at[7])
-    own_copy.start()
     row_ids = lax.broadcasted_iota(jnp.int32, (rows, size), 0) + f * rows
     bases = [table[f, share, me] for share in range(len(SHARES))]
 
@@ -282,24 +280,13 @@
 
     lax.fori_loop(0, lax.div(n_groups + 2 * GROUPS - 1, 2 * GROUPS), step, 0)
 
-    copies = [own_copy]
-    for share in range(len(SHARES)):
-        copy = pltpu.make_async_copy(accs[share].at[pl.ds(0, half)], keeps[share], sem.at[share, 0])
-        copy.start()
-        copies.append(copy)
     chunk = chunk_of(parts)
     pieces = half // chunk
     for piece in range(pieces):
         for share, (start, length) in enumerate(SHARES):
             acc = accs[share]
             first = half + (pieces - 1 - piece) * chunk
-            out = sends[share].at[piece]
-            encode(lambda j: acc[first + j], chunk, length, out, peak, inv)
-            copy = pltpu.make_async_copy(out, messages[share].at[piece], sem.at[share, 1 + piece])
-            copy.start()
-            copies.append(copy)
-    for copy in copies:
-        copy.wait()
+            encode(lambda j: acc[first + j], chunk, length, sends[share].at[piece], peak, inv)
 
 
 def first_layer(parts, dst, src, limit, features, other, wn, wn_other, ws, ws_other, tiles):
@@ -318,26 +305,22 @@
     return pl.pallas_call(
         functools.partial(first_layer_kernel, parts),
         in_specs=[scalars] * 4 + [anywhere] * 7,
-        out_specs=[anywhere] * 7,
-        scratch_shapes=[pltpu.VMEM((parts, n, width), jnp.float32) for n in lengths]
-        + [pltpu.VMEM(shape, jnp.int32) for shape in message]
-        + [pltpu.VMEM(a.shape, a.dtype) for a in operands]
+        out_specs=[pl.BlockSpec(memory_space=pltpu.VMEM)] * 7,
+        scratch_shapes=[pltpu.VMEM(a.shape, a.dtype) for a in operands]
         + [
             pltpu.VMEM((n_tiles, rows, size), tiles.dtype),
             pltpu.SMEM((blocks, n_tiles + GROUP), jnp.int32),
             pltpu.SMEM((blocks,), jnp.int32),
             pltpu.SMEM((3, n_tiles // GROUP + blocks + 3 * GROUPS), jnp.int32),
             pltpu.VMEM((2, GROUPS * GROUP * rows, 2 * features.shape[1]), jnp.bfloat16),
-            pltpu.VMEM((rows, width), jnp.float32),
             pltpu.VMEM((max(chunk, 8), width // 2), jnp.float32),
             pltpu.VMEM((max(chunk, 8), width // 2), jnp.float32),
-            pltpu.SemaphoreType.DMA((len(SHARES), 1 + pieces)),
-            pltpu.SemaphoreType.DMA((8,)),
+            pltpu.SemaphoreType.DMA((7,)),
         ],
-        out_shape=[jax.ShapeDtypeStruct((half, n, width), jnp.float32) for n in lengths]
-        + [jax.ShapeDtypeStruct(shape, jnp.int32) for shape in message]
-        + [jax.ShapeDtypeStruct((rows, width), jnp.float32)],
-        compiler_params=pltpu.CompilerParams(vmem_limit_bytes=VMEM_LIMIT),
+        out_shape=[pltpu.VMEM((parts, n, width), jnp.float32) for n in lengths]
+        + [pltpu.VMEM(shape, jnp.int32) for shape in message]
+        + [pltpu.VMEM((rows, width), jnp.float32)],
+        compiler_params=pltpu.CompilerParams(vmem_limit_bytes=FIRST_VMEM),
         name="first_layer",
     )(jnp.asarray(slot_table(parts)), dst, src, limit, *operands, tiles)
 
@@ -349,7 +332,7 @@
     plans = [plan_of(parts, share) for share in range(n_shares)]
     n_stages = len(plans[0])
     keeps, messages = refs[0:3], refs[3:6]
-    own_ref, list_ref, count_ref, adj_ref, w_self_ref, w_neigh_ref, out_ref = refs[6:13]
+    own_ref, list_ref, count_hbm, adj_hbm, w_self_hbm, w_neigh_hbm, out_ref = refs[6:13]
     at = 13
     work = refs[at : at + 3]
     at += 3
@@ -361,7 +344,8 @@
         outgoing.append(refs[at : at + 3] if k > 0 else None)
         at += 3 if k > 0 else 0
     (peak, inv, scale, lists, onehot, hid_own, hid_other, rows_out, rows_in, part, part_other) = refs[at : at + 11]
-    local_sem, send_sem, recv_sem, pair_sem, rows_sem = refs[at + 11 :]
+    count_ref, adj_ref, w_self_ref, w_neigh_ref = refs[at + 11 : at + 15]
+    local_sem, send_sem, recv_sem, pair_sem, rows_sem = refs[at + 15 :]
 
     f = lax.axis_index("feat")
     me = lax.axis_index("dom")
@@ -400,13 +384,20 @@
             in_flight[0, share, 1, piece] = copy
     loads = []
     for share in range(n_shares):
-        copy = pltpu.make_async_copy(keeps[share], work[share], local_sem.at[share])
+        copy = pltpu.make_async_copy(keeps[share].at[pl.ds(0, parts // 2)], work[share], local_sem.at[share])
         copy.start()
         loads.append(copy)
 
     get_lists = pltpu.make_async_copy(list_ref.at[me], lists, local_sem.at[len(SHARES)])
     get_lists.start()
-    get_lists.wait()
+    loads.append(get_lists)
+    late = ((count_hbm, count_ref), (adj_hbm, adj_ref), (w_self_hbm, w_self_ref), (w_neigh_hbm, w_neigh_ref))
+    for k, (source, target) in enumerate(late):
+        copy = pltpu.make_async_copy(source, target, local_sem.at[len(SHARES) + 1 + k])
+        copy.start()
+        loads.append(copy)
+    for copy in loads:
+        copy.wait()
     slots = lists.shape[0]
     shape = lists.shape
     lanes = lax.broadcasted_iota(jnp.int32, shape, 1)
@@ -419,7 +410,7 @@
     at_y = [lax.rem(py + d, ny) * nx for d in range(ny)]
     at_z = [lax.rem(pz + d, nz) * (nx * ny) for d in range(nz)]
     receivers = []
-    for d in range(nz // 2):
+    for d in [0] + sorted(range(1, nz // 2), key=lambda d: -min(2 * d, nz - 2 * d)):
         by_parity = [jnp.where(f == odd, at_z[2 * d], at_z[2 * d + 1]) for odd in range(2)]
         for dy in range(ny):
             for dx in range(nx):
@@ -431,8 +422,6 @@
             column = jnp.sum(jnp.where(lanes == r, wanted, 0.0), axis=1, keepdims=True)
             pair.append(jnp.where(column == ids, 1.0, 0.0))
         onehot[i * slots : (i + 2) * slots, :] = jnp.concatenate(pair, axis=0).astype(jnp.bfloat16)
-    for copy in loads:
-        copy.wait()
 
     def absorb(k, share, mask, piece, low, high):
         bits, stay, pieces, size = plans[share][k]
@@ -511,7 +500,8 @@
             device_id_type=MESH,
         )
 
-    for i in range(1, len(receivers)):
+    near = nx * ny
+    for i in list(range(near, len(receivers))) + list(range(1, near)):
         to_receiver(i).start()
 
     @pl.when(f == 0)
@@ -566,7 +556,7 @@
     half = width // 2
     lengths = [length for _, length in SHARES]
     slots = lists.shape[1]
-    buffers = [pltpu.VMEM(a.shape, jnp.float32) for a in keeps]
+    buffers = [pltpu.VMEM((parts // 2,) + a.shape[1:], jnp.float32) for a in keeps]
     for first_stage in (0, 1):
         for k in range(first_stage, n_stages):
             for share, n in enumerate(lengths):
@@ -583,11 +573,15 @@
         pltpu.VMEM((parts, 2 * slots, half), jnp.bfloat16),
         pltpu.VMEM((adj.shape[0], width), jnp.float32),
         pltpu.VMEM((adj.shape[0], width), jnp.float32),
+        pltpu.VMEM(counts.shape, counts.dtype),
+        pltpu.VMEM(adj.shape, adj.dtype),
+        pltpu.VMEM(w_self.shape, w_self.dtype),
+        pltpu.VMEM(w_neigh.shape, w_neigh.dtype),
     ]
     numbers = max(sum((2 ** len(p[0]) - 1) * p[2] for p in plan) for plan in plans)
     dma = pltpu.SemaphoreType.DMA
     buffers += [
-        dma((len(SHARES) + 1,)),
+        dma((len(SHARES) + 5,)),
         dma((len(SHARES), numbers)),
         dma((len(SHARES), numbers)),
         dma((2, 2)),
@@ -596,11 +590,11 @@
     return pl.pallas_call(
         functools.partial(second_layer_kernel, parts),
         out_shape=jax.ShapeDtypeStruct((adj.shape[0], w_self.shape[0]), jnp.float32),
-        in_specs=[anywhere] * 6 + [whole, anywhere] + [whole] * 4,
+        in_specs=[whole] * 7 + [anywhere] * 5,
         out_specs=whole,
         scratch_shapes=buffers,
         compiler_params=pltpu.CompilerParams(
-            collective_id=1, has_side_effects=True, vmem_limit_bytes=VMEM_LIMIT
+            collective_id=1, has_side_effects=True, vmem_limit_bytes=SECOND_VMEM
         ),
         name="reduce_and_second_layer",
     )(*keeps, *messages, own, lists, counts, adj, w_self, w_neigh)

time: 85.4 us -> 80 us (0.937)
  Pallas kernels: 83.7 us -> 79.2 us
    pallas_call x1, Pallas kernels: 58.4 us -> 55.8 us  [second_layer(): pl.pallas_call(functools.partial(second_layer_kernel, parts), out_shape=j...]
    pallas_call x1, Pallas kernels: 18.6 us -> 16.7 us  [first_layer(): pl.pallas_call(functools.partial(first_layer_kernel, parts), in_specs=[sc...]
where the time goes in v4:
time: 80 us; the launch traced here: 79.9 us
  Pallas kernels  79.2 us (99%)
    pallas_call x1, Pallas kernels, second_layer(): pl.pallas_call(functools.partial(second_layer_kernel, parts), out_shape=j...  55.8 us
    pallas_call x1, Pallas kernels, first_layer(): pl.pallas_call(functools.partial(first_layer_kernel, parts), in_specs=[sc...  16.7 us
    pallas_call x1, Pallas kernels, swap(): pl.pallas_call(swap_kernel, out_shape=[jax.ShapeDtypeStruct(a.shape, a.dt...  6.67 us

profile of v4, /device:TPU:1, one launch (start us, length us, event | category | flops | bytes accessed | tf_op | source)
XLA Modules:
  0.0 79.9 jit_solution(1635168158102798365)
XLA Ops:
  0.0 6.7 %swap_halves.1 = (bf16[1024,512]{1,0:T(8,128)(2,1)}, bf16[512,256]{1,0:T(8,128)(2,1)}, bf16[512,256]{1,0:T(8,128)(2,1)}) custom-call(bf16[1024,512]{1,0:T(8,128)(2,1)} %refs_4_.1, bf16[512,256]{1,0:T(8,128)(2,1)} %refs_6_.1, bf16[512,256]{1,0:T(8,128)(2,1)} %refs_8_.2), custom_call_target="tpu_custom_call" | custom-call | tf_op jit(solution)/shard_map/swap_halves/pallas_call | solution.py:117
  6.7 0.0 copy-start
  6.7 0.0 copy-start.1
  6.7 0.0 copy-start.2
  6.7 0.0 copy-start.3
  6.7 0.0 copy-start.4
  6.7 16.7 %first_layer.1 = (f32[128,24,256]{2,1,0:T(8,128)S(1)}, f32[128,24,256]{2,1,0:T(8,128)S(1)}, f32[128,16,256]{2,1,0:T(8,128)S(1)}, s32[4,400,128]{2,1,0:T(8,128)S(...) custom-call(s32[2,3,128]{2,1,0:T(4,128)} %constant.2.clone.refs_0_, ...), custom_call_target="tpu_custom_call" | custom-call | tf_op jit(solution)/shard_map/first_layer/pallas_call | solution.py:305
  23.5 0.0 copy-done
  23.5 0.0 copy-done.1
  23.5 0.0 copy-done.2
  23.5 0.0 copy-done.3
  23.5 0.0 copy-done.4
  23.5 55.8 %reduce_and_second_layer.1 = f32[64,172]{1,0:T(8,128)S(1)} custom-call(f32[128,24,256]{2,1,0:T(8,128)S(1)} %get-tuple-element.18.refs_0_, f32[128,24,256]{2,1,0:T(8,128)S(1)} %get-tuple-element.19.refs_1_, f32[128,16,256]{2,1,0:T(8,128)S(1)} %get-tuple-element.20.refs_2_, s32[4,400,128]{2,1,0:T(8,128)S(1)} %get-tuple-element.21.refs_3_, ...), custom_call_target="tpu_custom_call" | custom-call | tf_op jit(solution)/shard_map/reduce_and_second_layer/pallas_call | solution.py:590
  79.3 0.6 copy.15
Async XLA Ops:
  6.7 16.8 %copy-start = (s32[128,128,8]{1,2,0:T(8,128)S(1)}, s32[128,128,8]{1,2,0:T(8,128)}, u32[]{:S(2)}) copy-start(s32[128,128,8]{1,2,0:T(8,128)} %param.20) | copy-start | bytes 1572868
  6.7 16.8 %copy-start.1 = (bf16[64,1152]{1,0:T(8,128)(2,1)S(1)}, bf16[64,1152]{1,0:T(8,128)(2,1)}, u32[]{:S(2)}) copy-start(bf16[64,1152]{1,0:T(8,128)(2,1)} %refs_9_.1) | copy-start | bytes 442372
  6.7 16.8 %copy-start.2 = (bf16[256,172]{0,1:T(8,128)(2,1)S(1)}, bf16[256,172]{0,1:T(8,128)(2,1)}, u32[]{:S(2)}) copy-start(bf16[256,172]{0,1:T(8,128)(2,1)} %param.23) | copy-start | bytes 264196
  6.7 16.8 %copy-start.3 = (bf16[256,172]{0,1:T(8,128)(2,1)S(1)}, bf16[256,172]{0,1:T(8,128)(2,1)}, u32[]{:S(2)}) copy-start(bf16[256,172]{0,1:T(8,128)(2,1)} %param.24) | copy-start | bytes 264196
  6.7 16.8 %copy-start.4 = (s32[128,128]{1,0:T(8,128)S(1)}, s32[128,128]{1,0:T(8,128)}, u32[]{:S(2)}) copy-start(s32[128,128]{1,0:T(8,128)} %refs_8_.3) | copy-start | bytes 196612

commit v5 on v4

--- a/solution.py
+++ b/solution.py
@@ -199,9 +199,16 @@
         at = count[s]
         order[s, at] = t
         count[s] = at + 1
+        clear(t)
         return carry
 
+    def clear(j):
+        for acc in accs:
+            acc[j] = jnp.zeros(acc.shape[1:], jnp.float32)
+
     lax.fori_loop(0, n_tiles, place, 0)
+    for j in range(n_tiles, parts):
+        clear(j)
 
     def groups_of(s, at):
         n = count[s]
@@ -220,12 +227,6 @@
         plan[1, n_groups + g] = 0
         plan[2, n_groups + g] = 0
 
-    def clear(j, carry):
-        for acc in accs:
-            acc[j] = jnp.zeros(acc.shape[1:], jnp.float32)
-        return carry
-
-    lax.fori_loop(0, parts, clear, 0, unroll=4)
     for copy in loads:
         copy.wait()
 
@@ -356,10 +357,10 @@
                 chosen = tuple(sorted(b for i, b in enumerate(bits) if mask >> (len(bits) - 1 - i) & 1))
                 if chosen not in partners:
                     partners[chosen] = chip_across(parts, me, f, chosen)
-    rows_in[...] = jnp.zeros_like(rows_in)
     barrier = pltpu.get_barrier_semaphore()
     for target in [{"feat": 1 - f}] + [{"dom": dom} for dom in partners.values()]:
         pl.semaphore_signal(barrier, inc=1, device_id=target, device_id_type=MESH)
+    rows_in[...] = jnp.zeros_like(rows_in)
     pl.semaphore_wait(barrier, 1 + len(partners))
 
     def message(k, share, mask, piece, src):
@@ -485,11 +486,6 @@
     mine, theirs = hid_own[...], hid_other[...]
     hidden = jnp.concatenate([jnp.where(f == 0, mine, theirs), jnp.where(f == 0, theirs, mine)], axis=0)
     width = hidden.shape[1] // 2
-    picked = jnp.dot(onehot[...], hidden, preferred_element_type=jnp.float32)
-    for i in range(len(receivers)):
-        block = picked[i * slots : (i + 1) * slots, :]
-        rows_out[i] = jnp.concatenate([block[:, :width], block[:, width:]], axis=0).astype(jnp.bfloat16)
-
     def to_receiver(i):
         return pltpu.make_async_remote_copy(
             src_ref=rows_out.at[i],
@@ -501,8 +497,15 @@
         )
 
     near = nx * ny
-    for i in list(range(near, len(receivers))) + list(range(1, near)):
-        to_receiver(i).start()
+    for first in list(range(near, len(receivers), near)) + [0]:
+        picked = jnp.dot(
+            onehot[first * slots : (first + near) * slots, :], hidden, preferred_element_type=jnp.float32
+        )
+        for i in range(first, first + near):
+            block = picked[(i - first) * slots : (i - first + 1) * slots, :]
+            rows_out[i] = jnp.concatenate([block[:, :width], block[:, width:]], axis=0).astype(jnp.bfloat16)
+        for i in range(max(first, 1), first + near):
+            to_receiver(i).start()
 
     @pl.when(f == 0)
     def _():

time: 80 us -> 79.5 us (level)
  no operation moved by 1% of the time
where the time goes in v5:
time: 79.5 us; the launch traced here: 79.4 us
  Pallas kernels  78.6 us (99%)
    pallas_call x1, Pallas kernels, second_layer(): pl.pallas_call(functools.partial(second_layer_kernel, parts), out_shape=j...  55.6 us
    pallas_call x1, Pallas kernels, first_layer(): pl.pallas_call(functools.partial(first_layer_kernel, parts), in_specs=[sc...  16.3 us
    pallas_call x1, Pallas kernels, swap(): pl.pallas_call(swap_kernel, out_shape=[jax.ShapeDtypeStruct(a.shape, a.dt...  6.67 us

profile of v5, /device:TPU:1, one launch (start us, length us, event | category | flops | bytes accessed | tf_op | source)
XLA Modules:
  0.0 79.4 jit_solution(9730797728423720303)
XLA Ops:
  0.0 6.7 %swap_halves.1 = (bf16[1024,512]{1,0:T(8,128)(2,1)}, bf16[512,256]{1,0:T(8,128)(2,1)}, bf16[512,256]{1,0:T(8,128)(2,1)}) custom-call(bf16[1024,512]{1,0:T(8,128)(2,1)} %refs_4_.1, bf16[512,256]{1,0:T(8,128)(2,1)} %refs_6_.1, bf16[512,256]{1,0:T(8,128)(2,1)} %refs_8_.2), custom_call_target="tpu_custom_call" | custom-call | tf_op jit(solution)/shard_map/swap_halves/pallas_call | solution.py:117
  6.7 0.0 copy-start
  6.7 0.0 copy-start.1
  6.7 0.0 copy-start.2
  6.7 0.0 copy-start.3
  6.7 0.0 copy-start.4
  6.7 16.3 %first_layer.1 = (f32[128,24,256]{2,1,0:T(8,128)S(1)}, f32[128,24,256]{2,1,0:T(8,128)S(1)}, f32[128,16,256]{2,1,0:T(8,128)S(1)}, s32[4,400,128]{2,1,0:T(8,128)S(...) custom-call(s32[2,3,128]{2,1,0:T(4,128)} %constant.2.clone.refs_0_, ...), custom_call_target="tpu_custom_call" | custom-call | tf_op jit(solution)/shard_map/first_layer/pallas_call | solution.py:306
  23.1 0.0 copy-done
  23.1 0.0 copy-done.1
  23.1 0.0 copy-done.2
  23.1 0.0 copy-done.3
  23.1 0.0 copy-done.4
  23.1 55.6 %reduce_and_second_layer.1 = f32[64,172]{1,0:T(8,128)S(1)} custom-call(f32[128,24,256]{2,1,0:T(8,128)S(1)} %get-tuple-element.18.refs_0_, f32[128,24,256]{2,1,0:T(8,128)S(1)} %get-tuple-element.19.refs_1_, f32[128,16,256]{2,1,0:T(8,128)S(1)} %get-tuple-element.20.refs_2_, s32[4,400,128]{2,1,0:T(8,128)S(1)} %get-tuple-element.21.refs_3_, ...), custom_call_target="tpu_custom_call" | custom-call | tf_op jit(solution)/shard_map/reduce_and_second_layer/pallas_call | solution.py:593
  78.7 0.6 copy.15
Async XLA Ops:
  6.7 16.4 %copy-start = (s32[128,128,8]{1,2,0:T(8,128)S(1)}, s32[128,128,8]{1,2,0:T(8,128)}, u32[]{:S(2)}) copy-start(s32[128,128,8]{1,2,0:T(8,128)} %param.20) | copy-start | bytes 1572868
  6.7 16.4 %copy-start.1 = (bf16[64,1152]{1,0:T(8,128)(2,1)S(1)}, bf16[64,1152]{1,0:T(8,128)(2,1)}, u32[]{:S(2)}) copy-start(bf16[64,1152]{1,0:T(8,128)(2,1)} %refs_9_.1) | copy-start | bytes 442372
  6.7 16.4 %copy-start.2 = (bf16[256,172]{0,1:T(8,128)(2,1)S(1)}, bf16[256,172]{0,1:T(8,128)(2,1)}, u32[]{:S(2)}) copy-start(bf16[256,172]{0,1:T(8,128)(2,1)} %param.23) | copy-start | bytes 264196
  6.7 16.4 %copy-start.3 = (bf16[256,172]{0,1:T(8,128)(2,1)S(1)}, bf16[256,172]{0,1:T(8,128)(2,1)}, u32[]{:S(2)}) copy-start(bf16[256,172]{0,1:T(8,128)(2,1)} %param.24) | copy-start | bytes 264196
  6.7 16.4 %copy-start.4 = (s32[128,128]{1,0:T(8,128)S(1)}, s32[128,128]{1,0:T(8,128)}, u32[]{:S(2)}) copy-start(s32[128,128]{1,0:T(8,128)} %refs_8_.3) | copy-start | bytes 196612

commit v6 on v5

--- a/solution.py
+++ b/solution.py
@@ -173,9 +173,9 @@
 def first_layer_kernel(parts, *refs):
     table, dst, src, limit = refs[:4]
     inputs = refs[4:11]
-    accs, sends, own = refs[11:14], refs[14:17], refs[17]
-    held = refs[18:25]
-    order, count, plan, gathered, peak, inv, load_sem = refs[25:]
+    accs, own = refs[11:14], refs[14]
+    held = refs[15:22]
+    order, count, plan, gathered, load_sem = refs[22:]
     xa, xb, wa, wb, sa, sb, tiles = held
     f, me = lax.axis_index("feat"), lax.axis_index("dom")
     n_tiles, rows, size = tiles.shape
@@ -281,32 +281,20 @@
 
     lax.fori_loop(0, lax.div(n_groups + 2 * GROUPS - 1, 2 * GROUPS), step, 0)
 
-    chunk = chunk_of(parts)
-    pieces = half // chunk
-    for piece in range(pieces):
-        for share, (start, length) in enumerate(SHARES):
-            acc = accs[share]
-            first = half + (pieces - 1 - piece) * chunk
-            encode(lambda j: acc[first + j], chunk, length, sends[share].at[piece], peak, inv)
-
 
 def first_layer(parts, dst, src, limit, features, other, wn, wn_other, ws, ws_other, tiles):
     n_tiles, size, _ = tiles.shape
     rows = size // 2
     width = wn.shape[1]
-    half = parts // 2
-    chunk = chunk_of(parts)
-    pieces = half // chunk
     scalars = pl.BlockSpec(memory_space=pltpu.SMEM)
     anywhere = pl.BlockSpec(memory_space=pl.ANY)
     lengths = [length for _, length in SHARES]
-    message = [(pieces, chunk * n + chunk, width // 2) for n in lengths]
     operands = (features, other, wn, wn_other, ws, ws_other)
     blocks = features.shape[0] // size
     return pl.pallas_call(
         functools.partial(first_layer_kernel, parts),
         in_specs=[scalars] * 4 + [anywhere] * 7,
-        out_specs=[pl.BlockSpec(memory_space=pltpu.VMEM)] * 7,
+        out_specs=[pl.BlockSpec(memory_space=pltpu.VMEM)] * 4,
         scratch_shapes=[pltpu.VMEM(a.shape, a.dtype) for a in operands]
         + [
             pltpu.VMEM((n_tiles, rows, size), tiles.dtype),
@@ -314,12 +302,9 @@
             pltpu.SMEM((blocks,), jnp.int32),
             pltpu.SMEM((3, n_tiles // GROUP + blocks + 3 * GROUPS), jnp.int32),
             pltpu.VMEM((2, GROUPS * GROUP * rows, 2 * features.shape[1]), jnp.bfloat16),
-            pltpu.VMEM((max(chunk, 8), width // 2), jnp.float32),
-            pltpu.VMEM((max(chunk, 8), width // 2), jnp.float32),
             pltpu.SemaphoreType.DMA((7,)),
         ],
         out_shape=[pltpu.VMEM((parts, n, width), jnp.float32) for n in lengths]
-        + [pltpu.VMEM(shape, jnp.int32) for shape in message]
         + [pltpu.VMEM((rows, width), jnp.float32)],
         compiler_params=pltpu.CompilerParams(vmem_limit_bytes=FIRST_VMEM),
         name="first_layer",
@@ -332,11 +317,10 @@
     n_shares = len(SHARES)
     plans = [plan_of(parts, share) for share in range(n_shares)]
     n_stages = len(plans[0])
-    keeps, messages = refs[0:3], refs[3:6]
-    own_ref, list_ref, count_hbm, adj_hbm, w_self_hbm, w_neigh_hbm, out_ref = refs[6:13]
-    at = 13
-    work = refs[at : at + 3]
-    at += 3
+    keeps = refs[0:3]
+    own_ref, list_ref, count_hbm, adj_hbm, w_self_hbm, w_neigh_hbm, out_ref = refs[3:10]
+    work, messages = refs[10:13], refs[13:16]
+    at = 16
     receive, outgoing = [], []
     for k in range(n_stages):
         receive.append(refs[at : at + 3])
@@ -361,6 +345,15 @@
     for target in [{"feat": 1 - f}] + [{"dom": dom} for dom in partners.values()]:
         pl.semaphore_signal(barrier, inc=1, device_id=target, device_id_type=MESH)
     rows_in[...] = jnp.zeros_like(rows_in)
+
+    def encode_first(piece):
+        for share, (_, length) in enumerate(SHARES):
+            bits, stay, pieces, size = plans[share][0]
+            first = stay + (pieces - 1 - piece) * size
+            keep = keeps[share]
+            encode(lambda j: keep[first + j], size, length, messages[share].at[piece], peak, inv)
+
+    encode_first(0)
     pl.semaphore_wait(barrier, 1 + len(partners))
 
     def message(k, share, mask, piece, src):
@@ -379,6 +372,8 @@
 
     in_flight = {}
     for piece in range(plans[0][0][2]):
+        if piece > 0:
+            encode_first(piece)
         for share in range(n_shares):
             copy = message(0, share, 1, piece, messages[share].at[piece])
             copy.start()
@@ -550,7 +545,7 @@
         copy.wait_send()
 
 
-def second_layer(parts, keeps, messages, own, lists, counts, adj, w_self, w_neigh):
+def second_layer(parts, keeps, own, lists, counts, adj, w_self, w_neigh):
     plans = [plan_of(parts, share) for share in range(len(SHARES))]
     n_stages = len(plans[0])
     whole = pl.BlockSpec(memory_space=pltpu.VMEM)
@@ -560,8 +555,8 @@
     lengths = [length for _, length in SHARES]
     slots = lists.shape[1]
     buffers = [pltpu.VMEM((parts // 2,) + a.shape[1:], jnp.float32) for a in keeps]
-    for first_stage in (0, 1):
-        for k in range(first_stage, n_stages):
+    for first_stage in (None, 0, 1):
+        for k in range(1) if first_stage is None else range(first_stage, n_stages):
             for share, n in enumerate(lengths):
                 bits, stay, pieces, size = plans[share][k]
                 buffers.append(pltpu.VMEM(((2 ** len(bits) - 1) * pieces, size * n + size, half), jnp.int32))
@@ -593,14 +588,14 @@
     return pl.pallas_call(
         functools.partial(second_layer_kernel, parts),
         out_shape=jax.ShapeDtypeStruct((adj.shape[0], w_self.shape[0]), jnp.float32),
-        in_specs=[whole] * 7 + [anywhere] * 5,
+        in_specs=[whole] * 4 + [anywhere] * 5,
         out_specs=whole,
         scratch_shapes=buffers,
         compiler_params=pltpu.CompilerParams(
             collective_id=1, has_side_effects=True, vmem_limit_bytes=SECOND_VMEM
         ),
         name="reduce_and_second_layer",
-    )(*keeps, *messages, own, lists, counts, adj, w_self, w_neigh)
+    )(*keeps, own, lists, counts, adj, w_self, w_neigh)
 
 
 def body(
@@ -632,7 +627,7 @@
         ws_other,
         tile_weight,
     )
-    return second_layer(parts, results[:3], results[3:6], results[6], send_list.transpose(0, 2, 1), send_count, adj_two, w_self2.T, w_neigh2.T)
+    return second_layer(parts, results[:3], results[3], send_list.transpose(0, 2, 1), send_count, adj_two, w_self2.T, w_neigh2.T)
 
 
 def solution(mesh):

time: 79.5 us -> 79 us (level)
    pallas_call x1, Pallas kernels: 16.3 us -> 15.5 us  [first_layer(): pl.pallas_call(functools.partial(first_layer_kernel, parts), in_specs=[sc...]
where the time goes in v6:
time: 79 us; the launch traced here: 78.7 us
  Pallas kernels  77.9 us (99%)
    pallas_call x1, Pallas kernels, second_layer(): pl.pallas_call(functools.partial(second_layer_kernel, parts), out_shape=j...  55.7 us
    pallas_call x1, Pallas kernels, first_layer(): pl.pallas_call(functools.partial(first_layer_kernel, parts), in_specs=[sc...  15.5 us
    pallas_call x1, Pallas kernels, swap(): pl.pallas_call(swap_kernel, out_shape=[jax.ShapeDtypeStruct(a.shape, a.dt...  6.67 us

profile of v6, /device:TPU:1, one launch (start us, length us, event | category | flops | bytes accessed | tf_op | source)
XLA Modules:
  0.0 78.7 jit_solution(2454888565665056812)
XLA Ops:
  0.0 6.7 %swap_halves.1 = (bf16[1024,512]{1,0:T(8,128)(2,1)}, bf16[512,256]{1,0:T(8,128)(2,1)}, bf16[512,256]{1,0:T(8,128)(2,1)}) custom-call(bf16[1024,512]{1,0:T(8,128)(2,1)} %refs_4_.1, bf16[512,256]{1,0:T(8,128)(2,1)} %refs_6_.2, bf16[512,256]{1,0:T(8,128)(2,1)} %refs_8_.1), custom_call_target="tpu_custom_call" | custom-call | tf_op jit(solution)/shard_map/swap_halves/pallas_call | solution.py:117
  6.7 0.0 copy-start
  6.7 0.0 copy-start.1
  6.7 0.0 copy-start.2
  6.7 0.0 copy-start.3
  6.7 0.0 copy-start.4
  6.7 15.5 %first_layer.1 = (f32[128,24,256]{2,1,0:T(8,128)S(1)}, f32[128,24,256]{2,1,0:T(8,128)S(1)}, f32[128,16,256]{2,1,0:T(8,128)S(1)}, f32[64,256]{1,0:T(8,128)S(1)}) custom-call(s32[2,3,128]{2,1,0:T(4,128)} %constant.2.clone.refs_0_, s32[128]{0:T(128)} %refs_1_.1, s32[128]{0:T(128)} %refs_2_.1, s32[128]{0:T(128)} %refs_3_.1, bf16[1024,512]{1,0:T(8,128)(2,1)} %refs_4_.1, ...), custom_call_target="tpu_custom_call" | custom-call | tf_op jit(solution)/shard_map/first_layer/pallas_call | solution.py:294
  22.3 0.0 copy-done
  22.3 0.0 copy-done.1
  22.3 0.0 copy-done.2
  22.3 0.0 copy-done.3
  22.3 0.0 copy-done.4
  22.3 55.7 %reduce_and_second_layer.1 = f32[64,172]{1,0:T(8,128)S(1)} custom-call(f32[128,24,256]{2,1,0:T(8,128)S(1)} %get-tuple-element.15.refs_0_, f32[128,24,256]{2,1,0:T(8,128)S(1)} %get-tuple-element.16.refs_1_, f32[128,16,256]{2,1,0:T(8,128)S(1)} %get-tuple-element.17.refs_2_, f32[64,256]{1,0:T(8,128)S(1)} %get-tuple-element.18.refs_3_, ...), custom_call_target="tpu_custom_call" | custom-call | tf_op jit(solution)/shard_map/reduce_and_second_layer/pallas_call | solution.py:588
  78.1 0.6 copy.15
Async XLA Ops:
  6.7 15.6 %copy-start = (s32[128,128,8]{1,2,0:T(8,128)S(1)}, s32[128,128,8]{1,2,0:T(8,128)}, u32[]{:S(2)}) copy-start(s32[128,128,8]{1,2,0:T(8,128)} %param.20) | copy-start | bytes 1572868
  6.7 15.6 %copy-start.1 = (bf16[64,1152]{1,0:T(8,128)(2,1)S(1)}, bf16[64,1152]{1,0:T(8,128)(2,1)}, u32[]{:S(2)}) copy-start(bf16[64,1152]{1,0:T(8,128)(2,1)} %refs_6_.3) | copy-start | bytes 442372
  6.7 15.6 %copy-start.2 = (bf16[256,172]{0,1:T(8,128)(2,1)S(1)}, bf16[256,172]{0,1:T(8,128)(2,1)}, u32[]{:S(2)}) copy-start(bf16[256,172]{0,1:T(8,128)(2,1)} %param.23) | copy-start | bytes 264196
  6.7 15.6 %copy-start.3 = (bf16[256,172]{0,1:T(8,128)(2,1)S(1)}, bf16[256,172]{0,1:T(8,128)(2,1)}, u32[]{:S(2)}) copy-start(bf16[256,172]{0,1:T(8,128)(2,1)} %param.24) | copy-start | bytes 264196
  6.7 15.6 %copy-start.4 = (s32[128,128]{1,0:T(8,128)S(1)}, s32[128,128]{1,0:T(8,128)}, u32[]{:S(2)}) copy-start(s32[128,128]{1,0:T(8,128)} %refs_5_.1) | copy-start | bytes 196612

commit v7 on v6

--- a/solution.py
+++ b/solution.py
@@ -206,7 +206,7 @@
         for acc in accs:
             acc[j] = jnp.zeros(acc.shape[1:], jnp.float32)
 
-    lax.fori_loop(0, n_tiles, place, 0)
+    lax.fori_loop(0, n_tiles, place, 0, unroll=8)
     for j in range(n_tiles, parts):
         clear(j)
 
@@ -530,13 +530,16 @@
         arrived[:, k * slots : (k + 1) * slots, :].reshape(parts * slots, width).astype(jnp.bfloat16)
         for k in range(2)
     ]
+    share_part = []
     for k in range(2):
         part[:, k * width : (k + 1) * width] = jnp.dot(
             adj_ref[:, n_own:], pool[k], preferred_element_type=jnp.float32
         )
-    share_part = to_pair(part, part_other, 1)
-    share_part.start()
-    share_part.wait()
+        at = (slice(None), pl.ds(k * width, width))
+        share_part.append(to_pair(part.at[at], part_other.at[at], 1 + k))
+        share_part[k].start()
+    for copy in share_part:
+        copy.wait()
     aggregate = (part[...] + part_other[...] + own_total).astype(jnp.bfloat16)
     out_ref[...] = self_logits + lax.dot_general(
         aggregate, w_neigh_ref[...], (((1,), (1,)), ((), ())), preferred_element_type=jnp.float32
@@ -582,7 +585,7 @@
         dma((len(SHARES) + 5,)),
         dma((len(SHARES), numbers)),
         dma((len(SHARES), numbers)),
-        dma((2, 2)),
+        dma((2, 3)),
         dma((2,)),
     ]
     return pl.pallas_call(

time: 79 us -> 79.2 us (level)
  no operation moved by 1% of the time
where the time goes in v7:
time: 79.2 us; the launch traced here: 79.3 us
  Pallas kernels  78.5 us (99%)
    pallas_call x1, Pallas kernels, second_layer(): pl.pallas_call(functools.partial(second_layer_kernel, parts), out_shape=j...  56.3 us
    pallas_call x1, Pallas kernels, first_layer(): pl.pallas_call(functools.partial(first_layer_kernel, parts), in_specs=[sc...  15.6 us
    pallas_call x1, Pallas kernels, swap(): pl.pallas_call(swap_kernel, out_shape=[jax.ShapeDtypeStruct(a.shape, a.dt...  6.67 us

profile of v7, /device:TPU:1, one launch (start us, length us, event | category | flops | bytes accessed | tf_op | source)
XLA Modules:
  0.0 79.3 jit_solution(16567063333895348909)
XLA Ops:
  0.0 6.7 %swap_halves.1 = (bf16[1024,512]{1,0:T(8,128)(2,1)}, bf16[512,256]{1,0:T(8,128)(2,1)}, bf16[512,256]{1,0:T(8,128)(2,1)}) custom-call(bf16[1024,512]{1,0:T(8,128)(2,1)} %refs_4_.1, bf16[512,256]{1,0:T(8,128)(2,1)} %refs_6_.2, bf16[512,256]{1,0:T(8,128)(2,1)} %refs_8_.1), custom_call_target="tpu_custom_call" | custom-call | tf_op jit(solution)/shard_map/swap_halves/pallas_call | solution.py:117
  6.7 0.0 copy-start
  6.7 0.0 copy-start.1
  6.7 0.0 copy-start.2
  6.7 0.0 copy-start.3
  6.7 0.0 copy-start.4
  6.7 15.6 %first_layer.1 = (f32[128,24,256]{2,1,0:T(8,128)S(1)}, f32[128,24,256]{2,1,0:T(8,128)S(1)}, f32[128,16,256]{2,1,0:T(8,128)S(1)}, f32[64,256]{1,0:T(8,128)S(1)}) custom-call(s32[2,3,128]{2,1,0:T(4,128)} %constant.2.clone.refs_0_, s32[128]{0:T(128)} %refs_1_.1, s32[128]{0:T(128)} %refs_2_.1, s32[128]{0:T(128)} %refs_3_.1, bf16[1024,512]{1,0:T(8,128)(2,1)} %refs_4_.1, ...), custom_call_target="tpu_custom_call" | custom-call | tf_op jit(solution)/shard_map/first_layer/pallas_call | solution.py:294
  22.3 0.0 copy-done
  22.3 0.0 copy-done.1
  22.3 0.0 copy-done.2
  22.3 0.0 copy-done.3
  22.4 0.0 copy-done.4
  22.4 56.3 %reduce_and_second_layer.1 = f32[64,172]{1,0:T(8,128)S(1)} custom-call(f32[128,24,256]{2,1,0:T(8,128)S(1)} %get-tuple-element.15.refs_0_, f32[128,24,256]{2,1,0:T(8,128)S(1)} %get-tuple-element.16.refs_1_, f32[128,16,256]{2,1,0:T(8,128)S(1)} %get-tuple-element.17.refs_2_, f32[64,256]{1,0:T(8,128)S(1)} %get-tuple-element.18.refs_3_, ...), custom_call_target="tpu_custom_call" | custom-call | tf_op jit(solution)/shard_map/reduce_and_second_layer/pallas_call | solution.py:591
  78.7 0.6 copy.15
Async XLA Ops:
  6.7 15.6 %copy-start = (s32[128,128,8]{1,2,0:T(8,128)S(1)}, s32[128,128,8]{1,2,0:T(8,128)}, u32[]{:S(2)}) copy-start(s32[128,128,8]{1,2,0:T(8,128)} %param.20) | copy-start | bytes 1572868
  6.7 15.6 %copy-start.1 = (bf16[64,1152]{1,0:T(8,128)(2,1)S(1)}, bf16[64,1152]{1,0:T(8,128)(2,1)}, u32[]{:S(2)}) copy-start(bf16[64,1152]{1,0:T(8,128)(2,1)} %refs_6_.3) | copy-start | bytes 442372
  6.7 15.6 %copy-start.2 = (bf16[256,172]{0,1:T(8,128)(2,1)S(1)}, bf16[256,172]{0,1:T(8,128)(2,1)}, u32[]{:S(2)}) copy-start(bf16[256,172]{0,1:T(8,128)(2,1)} %param.23) | copy-start | bytes 264196
  6.7 15.6 %copy-start.3 = (bf16[256,172]{0,1:T(8,128)(2,1)S(1)}, bf16[256,172]{0,1:T(8,128)(2,1)}, u32[]{:S(2)}) copy-start(bf16[256,172]{0,1:T(8,128)(2,1)} %param.24) | copy-start | bytes 264196
  6.7 15.6 %copy-start.4 = (s32[128,128]{1,0:T(8,128)S(1)}, s32[128,128]{1,0:T(8,128)}, u32[]{:S(2)}) copy-start(s32[128,128]{1,0:T(8,128)} %refs_5_.1) | copy-start | bytes 196612
